TPU v7x, 128 devices: a whole 4x4x4 slice. The times are simulated.
128 devices in a mesh: dp: 4 (over z), seq: 32 (over x, y, core).
Axes of the slice: x: 4, y: 4, z: 4, core: 2. Of those that a mesh axis runs over, the one named last changes fastest.
Arguments:
- tokens: bfloat16 [8192, 4096], P(('dp', 'seq')), may hold values from -240 to 240
- grad_in: bfloat16 [8192, 4096], P(('dp', 'seq')), may hold values from -6 to 6
- enc_store: bfloat16 [512, 128, 896], P(('dp', 'seq')), may hold values from -6 to 6
- nbr_owner: int32 [4, 64], replicated, may hold values from 0 to 3
- nbr_row: int32 [4, 64], replicated, may hold values from 0 to 3
- w_query: bfloat16 [4096, 4096], P(None, 'seq'), may hold values from -0.09375 to 0.09375
- w_key: bfloat16 [896, 4096], P(None, 'seq'), may hold values from -0.1875 to 0.1875
- w_value: bfloat16 [896, 4096], P(None, 'seq'), may hold values from -0.1875 to 0.1875
- w_out: bfloat16 [4096, 4096], P('seq'), may hold values from -0.09375 to 0.09375
Outputs:
- grad_tokens: bfloat16 [8192, 4096], P(('dp', 'seq'))
- grad_query: float32 [4096, 4096], P(None, 'seq')
- grad_key: float32 [896, 4096], P(None, 'seq')
- grad_value: float32 [896, 4096], P(None, 'seq')
- grad_out: float32 [4096, 4096], P('seq')
All inputs are finite; a program needn't handle non-finite values.
Results may differ from a plain program's by a relative error of at most 0.023.
The roundings to bfloat16 on the way count: a program that leaves them out, or rounds other values in their place, can miss the bound.
Values may be sent and summed in bfloat16 or wider, within the bound.
No kernel may reach another device: no remote copies, remote signals or barrier semaphores. Data moves between devices by JAX's collectives and lax.ppermute only.
A program may use at most 192 MiB of HBM per device.

v0:
```python
import math

import jax
import jax.numpy as jnp
from jax import lax
from jax.sharding import PartitionSpec as P

DH = 128
ENC = 896
STRETCH = 64
NBRS = 2
NBR_LEN = 128


def shift_rows(array_in, margin):
    filler = jnp.zeros((margin,) + array_in.shape[1:], array_in.dtype)
    return jnp.concatenate([array_in[margin:], filler], 0)


def unshift_rows(array_in, margin):
    filler = jnp.zeros((margin,) + array_in.shape[1:], array_in.dtype)
    return jnp.concatenate([filler, array_in[: array_in.shape[0] - margin]], 0)


def inner(left, right):
    return lax.dot_general(
        left, right, (((0,), (0,)), ((), ())), preferred_element_type=jnp.float32
    )


def shards(tokens, grad_in, enc_store, nbr_owner, nbr_row, w_query, w_key, w_value, w_out):
    batch_index = lax.axis_index("dp")
    column = lax.axis_index("seq")
    n_dp = lax.axis_size("dp")
    n_seq = lax.axis_size("seq")
    shard_rows = tokens.shape[0]
    seq_tokens = shard_rows * n_seq
    slot_count = shard_rows * NBRS // STRETCH
    store_count = enc_store.shape[0]
    head_cols = w_query.shape[1]
    head_count = head_cols // DH
    stretches = seq_tokens // STRETCH
    key_span = NBRS * NBR_LEN
    inv_root = 1.0 / math.sqrt(DH)
    margin = STRETCH - 1
    owners = lax.dynamic_slice_in_dim(nbr_owner, column * slot_count, slot_count, 1)
    row_ids = lax.dynamic_slice_in_dim(nbr_row, column * slot_count, slot_count, 1)
    wanted = (owners == batch_index)[:, :, None] & (
        row_ids[:, :, None] == jnp.arange(store_count, dtype=jnp.int32)[None, None, :]
    )
    picker = wanted.astype(jnp.bfloat16).reshape(n_dp * slot_count, store_count)
    outgoing = jnp.dot(
        picker, enc_store.reshape(store_count, NBR_LEN * ENC), preferred_element_type=jnp.float32
    )
    arrived = lax.all_to_all(
        outgoing.astype(jnp.bfloat16), "dp", split_axis=0, concat_axis=0, tiled=True
    )
    source = lax.dynamic_index_in_dim(owners, batch_index, 0, keepdims=False)
    selector = (source[None, :] == jnp.arange(n_dp, dtype=jnp.int32)[:, None]).astype(jnp.bfloat16)
    own_units = jnp.einsum(
        "os,osf->sf",
        selector,
        arrived.reshape(n_dp, slot_count, NBR_LEN * ENC),
        preferred_element_type=jnp.float32,
    ).astype(jnp.bfloat16)
    own_units = own_units.reshape(slot_count, NBR_LEN, ENC)
    w_pair = jnp.concatenate([w_key, w_value], 1)
    all_tokens = lax.all_gather(tokens, "seq", axis=0, tiled=True)
    query_rows = jnp.dot(all_tokens, w_query, preferred_element_type=jnp.float32).astype(
        jnp.bfloat16
    )
    neighbours = lax.all_gather(own_units, "seq", axis=0, tiled=True).reshape(-1, ENC)
    key_value = jnp.dot(neighbours, w_pair, preferred_element_type=jnp.float32).astype(jnp.bfloat16)
    q_blocks = shift_rows(query_rows, margin).reshape(stretches, STRETCH, head_count, DH)
    k_blocks = key_value[:, :head_cols].reshape(stretches, key_span, head_count, DH)
    v_blocks = key_value[:, head_cols:].reshape(stretches, key_span, head_count, DH)
    scores = (
        jnp.einsum("cqhd,ckhd->chqk", q_blocks, k_blocks, preferred_element_type=jnp.float32)
        * inv_root
    )
    attn_probs = jax.nn.softmax(scores, axis=-1)
    probs_low = attn_probs.astype(jnp.bfloat16)
    context = jnp.einsum(
        "chqk,ckhd->cqhd", probs_low, v_blocks, preferred_element_type=jnp.float32
    ).astype(jnp.bfloat16)
    context = unshift_rows(context.reshape(seq_tokens, head_cols), margin)
    portion = lax.all_gather(grad_in, "seq", axis=0, tiled=True)
    term_rows = lax.dot_general(
        portion, w_out, (((1,), (1,)), ((), ())), preferred_element_type=jnp.float32
    )
    out_sum = inner(context, portion)
    grad_context = term_rows
    grad_context = grad_context.astype(jnp.bfloat16)
    grad_blocks = shift_rows(grad_context, margin).reshape(stretches, STRETCH, head_count, DH)
    grad_probs = jnp.einsum(
        "cqhd,ckhd->chqk", grad_blocks, v_blocks, preferred_element_type=jnp.float32
    )
    grad_value_rows = jnp.einsum(
        "chqk,cqhd->ckhd", probs_low, grad_blocks, preferred_element_type=jnp.float32
    ).astype(jnp.bfloat16)
    row_dot = jnp.sum(grad_probs * attn_probs, axis=-1, keepdims=True)
    grad_scores = (attn_probs * (grad_probs - row_dot) * inv_root).astype(jnp.bfloat16)
    grad_query_rows = jnp.einsum(
        "chqk,ckhd->cqhd", grad_scores, k_blocks, preferred_element_type=jnp.float32
    ).astype(jnp.bfloat16)
    grad_query_rows = unshift_rows(grad_query_rows.reshape(seq_tokens, head_cols), margin)
    grad_key_rows = jnp.einsum(
        "chqk,cqhd->ckhd", grad_scores, q_blocks, preferred_element_type=jnp.float32
    ).astype(jnp.bfloat16)
    grad_pair = jnp.concatenate(
        [grad_key_rows.reshape(-1, head_cols), grad_value_rows.reshape(-1, head_cols)], 1
    )
    query_part = inner(all_tokens, grad_query_rows)
    pair_part = inner(neighbours, grad_pair)
    grad_tokens = lax.psum_scatter(
        lax.dot_general(
            grad_query_rows, w_query, (((1,), (1,)), ((), ())), preferred_element_type=jnp.float32
        ).astype(jnp.bfloat16),
        "seq",
        scatter_dimension=0,
        tiled=True,
    )
    grad_query, pair_sum, grad_out = lax.psum((query_part, pair_part, out_sum), "dp")
    return (grad_tokens, grad_query, pair_sum[:, :head_cols], pair_sum[:, head_cols:], grad_out)


def solution(mesh):
    in_specs = (
        P(("dp", "seq"), None),
        P(("dp", "seq"), None),
        P(("dp", "seq"), None, None),
        P(),
        P(),
        P(None, "seq"),
        P(None, "seq"),
        P(None, "seq"),
        P("seq", None),
    )
    out_specs = (
        P(("dp", "seq"), None),
        P(None, "seq"),
        P(None, "seq"),
        P(None, "seq"),
        P("seq", None),
    )
    return jax.shard_map(shards, mesh=mesh, in_specs=in_specs, out_specs=out_specs, check_vma=False)
```

profile of v0, /device:TPU:2, one launch (start us, length us, event | category | flops | bytes accessed | tf_op | source)
XLA Modules:
  0.0 592.9 jit_solution(8256766329620246865)
XLA Ops:
  7.2 0.8 dynamic-slice_compare_fusion
  9.0 1.9 copy.24
  11.5 2.4 all_to_all.6
  13.9 5.3 all-to-all-start
  20.1 22.6 %all-to-all-done = bf16[4,2,114688]{2,1,0:T(2,128)(2,1)S(1)} async-done(((bf16[4,2,114688]{2,1,0:T(2,128)(2,1)}), bf16[4,2,114688]{2,1,0:T(2,128)(2,1)S(1)}, u32[]{:S(2)}, u32[]{:S(2)}) %all-to-all-start) | async-done | bytes 1835040 | tf_op jit(solution)/shard_map/all_to_all | solution.py:55
  42.7 2.4 fusion.10
  48.5 65.5 %all-gather.4.cloned.1.call-done = bf16[64,128,896]{2,1,0:T(8,128)(2,1)} async-done(((bf16[2,128,896]{2,1,0:T(8,128)(2,1)}), bf16[64,128,896]{2,1,0:T(8,128)(2,1)}) %all-gather.4.cloned.1.call-update) | async-done | bytes 14680080 | tf_op jit(solution)/shard_map/all_gather | solution.py:72
  114.0 9.7 %convolution_convert_fusion.2 = bf16[8192,256]{1,0:T(8,128)(2,1)S(1)} fusion(bf16[8192,896]{1,0:T(8,128)(2,1)} %bitcast.77, bf16[896,128]{1,0:T(8,128)(2,1)S(1)} %copy-done.7, bf16[896,128]{1,0:T(8,128)(2,1)S(1)} %copy-done.8), kind=kOutput, calls=%fused_computation.4 | convolution fusion | flops 3761111040 | bytes 19333120 | tf_op jit(solution)/shard_map/dot_general | solution.py:73
  123.7 2.3 fusion.55
  126.0 62.2 %all-gather.6.cloned.1.call-done = bf16[2048,4096]{1,0:T(8,128)(2,1)} async-done(((bf16[64,4096]{1,0:T(8,128)(2,1)}), bf16[2048,4096]{1,0:T(8,128)(2,1)}) %all-gather.6.cloned.1.call-update) | async-done | bytes 16777232 | tf_op jit(solution)/shard_map/all_gather | solution.py:68
  188.2 8.8 %fusion.58 = bf16[2048,128]{1,0:T(8,128)(2,1)S(1)} fusion(bf16[2048,4096]{1,0:T(8,128)(2,1)} %all-gather.6.cloned.1.call-done, bf16[4096,128]{1,0:T(8,128)(2,1)S(1)} %copy-done), kind=kOutput, calls=%fused_computation.62 | convolution fusion | flops 2147483648 | bytes 18350080 | tf_op jit(solution)/shard_map/dot_general | solution.py:69
  198.1 2.0 fusion.57
  200.1 62.4 %all-gather.8.cloned.1.call-done = bf16[2048,4096]{1,0:T(8,128)(2,1)} async-done(((bf16[64,4096]{1,0:T(8,128)(2,1)}), bf16[2048,4096]{1,0:T(8,128)(2,1)}) %all-gather.8.cloned.1.call-update) | async-done | bytes 16777232 | tf_op jit(solution)/shard_map/all_gather | solution.py:87
  262.4 10.5 %fusion.60 = bf16[2048,128]{1,0:T(8,128)(2,1)S(1)} fusion(bf16[2048,4096]{1,0:T(8,128)(2,1)} %all-gather.8.cloned.1.call-done, bf16[128,4096]{1,0:T(8,128)(2,1)} %param.17), kind=kOutput, calls=%fused_computation.64 | convolution fusion | flops 2147483648 | bytes 18350080 | tf_op jit(solution)/shard_map/dot_general | solution.py:88
  273.9 6.0 %convolution_convert_fusion.3 = bf16[32,128,64]{1,2,0:T(8,128)(2,1)} fusion(bf16[32,256,128]{2,1,0:T(8,128)(2,1)} %bitcast.63, f32[32,64]{1,0:T(8,128)S(1)} %get-tuple-element.27, f32[32,64,256]{2,1,0:T(8,128)S(1)} %fusion.59), kind=kOutput, calls=%fused_computation.22 | convolution fusion | flops 136579328 | bytes 4726784 | tf_op jit(solution)/shard_map/chqk,ckhd->cqhd/dot_general | solution.py:83
  280.0 4.0 fusion.61
  284.0 6.4 %convert_bitcast_fusion = bf16[32,256,1,128]{1,3,0,2:T(8,128)(2,1)} fusion(bf16[32,64,128]{2,1,0:T(8,128)(2,1)} %bitcast.69, f32[32,64]{1,0:T(8,128)S(1)} %get-tuple-element.27, f32[32,64,256]{2,1,0:T(8,128)S(1)} %fusion.59), kind=kOutput, calls=%fused_computation.10 | convolution fusion | flops 137365760 | bytes 4726784 | tf_op jit(solution)/shard_map/chqk,cqhd->ckhd/dot_general | solution.py:98
  290.4 16.9 %convert_bitcast_fusion.1 = bf16[32,256,1,128]{1,3,0,2:T(8,128)(2,1)} fusion(bf16[32,64,128]{2,1,0:T(8,128)(2,1)} %bitcast.67, f32[32,64,256]{2,1,0:T(8,128)} %fusion.61, f32[32,64,256]{2,1,0:T(8,128)} %get-tuple-element.28, f32[32,64]{1,0:T(8,128)S(1)} %get-tuple-element.27), kind=kOutput, calls=%fused_computation.11 | convolution fusion | flops 138938624 | bytes 6823936 | tf_op jit(solution)/shard_map/chqk,cqhd->ckhd/dot_general | solution.py:107
  307.3 15.5 %fusion.17 = bf16[32,128,64]{1,2,0:T(8,128)(2,1)} fusion(bf16[32,256,128]{2,1,0:T(8,128)(2,1)S(1)} %bitcast.62, f32[32,64,256]{2,1,0:T(8,128)} %fusion.61, f32[32,64,256]{2,1,0:T(8,128)} %get-tuple-element.28, f32[32,64]{1,0:T(8,128)S(1)} %get-tuple-element.27), kind=kOutput, calls=%fused_computation.21 | convolution fusion | flops 138152192 | bytes 6823936 | tf_op jit(solution)/shard_map/chqk,ckhd->cqhd/dot_general | solution.py:103
  322.8 1.8 slice.39
  324.6 4.2 copy.18
  328.8 2.8 copy.19
  331.7 1.1 slice.36
  332.8 11.5 %fusion.2 = f32[896,256]{1,0:T(8,128)} fusion(bf16[8192,896]{1,0:T(8,128)(2,1)} %bitcast.78, bf16[8192,128]{1,0:T(8,128)(2,1)} %bitcast.71, bf16[8192,128]{1,0:T(8,128)(2,1)} %bitcast.70), kind=kOutput, calls=%fused_computation.6 | convolution fusion | flops 3766484992 | bytes 19791872 | tf_op jit(solution)/shard_map/dot_general | solution.py:26
  344.3 9.6 %fusion.23 = f32[128,4096]{1,0:T(8,128)} fusion(bf16[2048,4096]{1,0:T(8,128)(2,1)} %all-gather.8.cloned.1.call-done, bf16[1985,128]{1,0:T(8,128)(2,1)S(1)} %copy-done.6), kind=kOutput, calls=%fused_computation.30 | convolution fusion | flops 2147483648 | bytes 19382528 | tf_op jit(solution)/shard_map/dot_general | solution.py:26
  354.0 3.7 convolution_bitcast_fusion
  357.8 8.4 %convolution_convert_fusion.1 = bf16[2048,4096]{1,0:T(8,128)(2,1)} fusion(bf16[4096,128]{1,0:T(8,128)(2,1)S(1)} %copy-done, bf16[1985,128]{1,0:T(8,128)(2,1)S(1)} %slice.36), kind=kOutput, calls=%fused_computation.3 | convolution fusion | flops 2155872256 | bytes 18333952 | tf_op jit(solution)/shard_map/dot_general | solution.py:116
  366.2 99.6 %all-reduce.7.cloned.1.call-done = (f32[4096,128]{0,1:T(8,128)}, f32[896,256]{1,0:T(8,128)}, f32[128,4096]{1,0:T(8,128)}) async-done(((f32[4096,128]{0,1:T(8,128)}, f32[896,256]{1,0:T(8,128)}, f32[128,4096]{1,0:T(8,128)}), (f32[4096,128]{0,1:T(8,128)}, f32[896,256]{1,0:T(8,128)}, f32[128,4096]{1,0:T(8,128)})) %all-reduce.7.cloned.1.call-update) | async-done | bytes 5111824 | tf_op jit(solution)/shard_map/psum | solution.py:123
  465.8 3.0 copy.20
  468.8 2.1 fusion.56
  470.9 113.9 %reduce-scatter.2.cloned.1.call-done = bf16[64,4096]{1,0:T(8,128)(2,1)} async-done(((bf16[2048,4096]{1,0:T(8,128)(2,1)}), bf16[64,4096]{1,0:T(8,128)(2,1)}) %reduce-scatter.2.cloned.1.call-update) | async-done | bytes 524304 | tf_op jit(solution)/shard_map/reduce_scatter | solution.py:115
  584.8 1.3 copy.35
  (51 shorter events, 7.9 us)
Async XLA Ops:
  7.2 181.1 %copy-start = (bf16[4096,128]{1,0:T(8,128)(2,1)S(1)}, bf16[4096,128]{1,0:T(8,128)(2,1)}, u32[]{:S(2)}) copy-start(bf16[4096,128]{1,0:T(8,128)(2,1)} %param.14) | copy-start | bytes 3145732
  13.9 28.8 %all-to-all-start = ((bf16[4,2,114688]{2,1,0:T(2,128)(2,1)}), bf16[4,2,114688]{2,1,0:T(2,128)(2,1)S(1)}, u32[]{:S(2)}, u32[]{:S(2)}) async-start(bf16[4,2,114688]{2,1,0:T(2,128)(2,1)} %all_to_all.6), calls=%async_computation | async-start | bytes 3670016 | tf_op jit(solution)/shard_map/all_to_all | solution.py:55
  19.2 94.8 %all-gather.4.cloned.1.call-start = ((), (), s32[]{:S(2)}) async-start(), calls=%async_computation.2 | async-start | bytes 15138816 | tf_op jit(solution)/shard_map/all_gather | solution.py:72
  45.2 68.9 %copy-start.7 = (bf16[896,128]{1,0:T(8,128)(2,1)S(1)}, bf16[896,128]{1,0:T(8,128)(2,1)}, u32[]{:S(2)}) copy-start(bf16[896,128]{1,0:T(8,128)(2,1)} %param.16) | copy-start | bytes 688132
  45.2 68.9 %copy-start.8 = (bf16[896,128]{1,0:T(8,128)(2,1)S(1)}, bf16[896,128]{1,0:T(8,128)(2,1)}, u32[]{:S(2)}) copy-start(bf16[896,128]{1,0:T(8,128)(2,1)} %param.15) | copy-start | bytes 688132
  46.7 141.5 %all-gather.6.cloned.1.call-start = ((), (), s32[]{:S(2)}) async-start(), calls=%async_computation.3 | async-start | bytes 17301504 | tf_op jit(solution)/shard_map/all_gather | solution.py:68
  47.5 214.9 %all-gather.8.cloned.1.call-start = ((), (), s32[]{:S(2)}) async-start(), calls=%async_computation.4 | async-start | bytes 17301504 | tf_op jit(solution)/shard_map/all_gather | solution.py:87
  48.2 417.5 %all-reduce.7.cloned.1.call-start = ((), (), s32[]{:S(2)}) async-start(), calls=%async_computation.6 | async-start | bytes 10223616 | tf_op jit(solution)/shard_map/psum | solution.py:123
  188.2 9.0 %copy-start.1 = (bf16[8192,128]{1,0:T(8,128)(2,1)S(1)}, bf16[8192,128]{1,0:T(8,128)(2,1)}, u32[]{:S(2)}) copy-start(bf16[8192,128]{1,0:T(8,128)(2,1)} %get-tuple-element.24) | copy-start | bytes 6291460
  197.2 0.9 copy-start.3
  290.4 16.9 %copy-start.2 = (bf16[8192,128]{1,0:T(8,128)(2,1)S(1)}, bf16[8192,128]{1,0:T(8,128)(2,1)}, u32[]{:S(2)}) copy-start(bf16[8192,128]{1,0:T(8,128)(2,1)} %get-tuple-element.24) | copy-start | bytes 6291460
  324.6 4.2 copy-start.5
  332.8 11.6 %copy-start.6 = (bf16[1985,128]{1,0:T(8,128)(2,1)S(1)}, bf16[1985,128]{1,0:T(8,128)(2,1)}, u32[]{:S(2)}) copy-start(bf16[1985,128]{1,0:T(8,128)(2,1)} %slice.39) | copy-start | bytes 1524484
  332.8 21.2 %slice-start = ((s8[16777216]{0:T(1024)(128)(4,1)}), s8[4194304]{0:T(1024)(128)(4,1)S(1)}, s32[]{:S(2)}) async-start(s8[16777216]{0:T(1024)(128)(4,1)} %bitcast.59), calls=%async_computation.7 | async-start | bytes 8388608
  332.8 21.2 %slice-start.1 = ((s8[16777216]{0:T(1024)(128)(4,1)}), s8[4194304]{0:T(1024)(128)(4,1)S(1)}, s32[]{:S(2)}) async-start(s8[16777216]{0:T(1024)(128)(4,1)} %bitcast.59), calls=%async_computation.8 | async-start | bytes 8388608
  332.8 21.2 %slice-start.2 = ((s8[16777216]{0:T(1024)(128)(4,1)}), s8[4194304]{0:T(1024)(128)(4,1)S(1)}, s32[]{:S(2)}) async-start(s8[16777216]{0:T(1024)(128)(4,1)} %bitcast.59), calls=%async_computation.9 | async-start | bytes 8388608
  344.3 9.6 %slice-start.3 = ((s8[16777216]{0:T(1024)(128)(4,1)}), s8[4194304]{0:T(1024)(128)(4,1)S(1)}, s32[]{:S(2)}) async-start(s8[16777216]{0:T(1024)(128)(4,1)} %bitcast.59), calls=%async_computation.10 | async-start | bytes 8388608
  357.7 227.1 %reduce-scatter.2.cloned.1.call-start = ((), (), s32[]{:S(2)}) async-start(), calls=%async_computation.5 | async-start | bytes 17301504 | tf_op jit(solution)/shard_map/reduce_scatter | solution.py:115
  465.8 119.1 %copy-start.4 = (f32[128,4096]{1,0:T(8,128)S(1)}, f32[128,4096]{1,0:T(8,128)}, u32[]{:S(2)}) copy-start(f32[128,4096]{1,0:T(8,128)} %get-tuple-element.33) | copy-start | bytes 6291460
Sparse Core Ops, SparseCore 0:
  46.9 67.1 all-gather.3
  116.3 71.8 all-gather.5
  190.5 71.8 all-gather.7
  357.8 107.8 all-reduce.6
  470.1 114.6 reduce-scatter.1
where the time goes:
time: 599 us; the launch traced here: 593 us
  waiting for transfers between devices  428 us (71%)
  matrix products  115 us (19%)
  local copies, waits for them, and re-layouts  27.5 us (5%)
  between operations  14.1 us (2%)
    reduce_scatter x1, waiting for transfers between devices, shards(): lax.psum_scatter(lax.dot_general(grad_query_rows, w_query, (((1,), (1,)),...  114 us
    psum x1, waiting for transfers between devices, shards(): lax.psum((query_part, pair_part, out_sum), 'dp')  99.6 us
    all_gather x1, waiting for transfers between devices, shards(): lax.all_gather(own_units, 'seq', axis=0, tiled=True).reshape(-1, ENC)  65.5 us
    all_gather x1, waiting for transfers between devices, shards(): portion = lax.all_gather(grad_in, 'seq', axis=0, tiled=True)  62.4 us
    all_gather x1, waiting for transfers between devices, shards(): all_tokens = lax.all_gather(tokens, 'seq', axis=0, tiled=True)  62.2 us
    dot_general x3, matrix products, inner(): lax.dot_general(left, right, (((0,), (0,)), ((), ())), preferred_element_...  24.9 us
    all_to_all x1, waiting for transfers between devices, shards(): lax.all_to_all(outgoing.astype(jnp.bfloat16), 'dp', split_axis=0, concat_...  22.6 us
    dot_general x1, matrix products, shards(): jnp.einsum('chqk,cqhd->ckhd', grad_scores, q_blocks, preferred_element_ty...  16.9 us
  transfers between devices with their start and end apart: 6, of which 6 were waited for; matrix products, arithmetic and copies ran while one was open for 6% of the time, Pallas kernels for 0%

commit v1 on v0

v1 whole, which is shorter than its diff:
```python
import math

import jax
import jax.numpy as jnp
from jax import lax
from jax.experimental import pallas as pl
from jax.experimental.pallas import tpu as pltpu
from jax.sharding import Mesh, PartitionSpec as P

DH = 128
ENC = 896
STRETCH = 64
NBRS = 2
NBR_LEN = 128
SPAN = NBRS * NBR_LEN
HEADS = 4
EARLY, LATE = (2, 1), (3, 0)
BF = jnp.bfloat16
ROWS = ("x", "c")
SEQ = ("x", "y", "c")


def dot(left, right, dims):
    return lax.dot_general(left, right, (dims, ((), ())), preferred_element_type=jnp.float32)


def forward_kernel(place_ref, q_ref, n_ref, *refs):
    w_refs, (kv_ref, probs_ref, ctx_ref) = refs[:HEADS], refs[-3:]
    heads = range(HEADS)
    inv_root = 1.0 / math.sqrt(DH)
    n = n_ref[...]
    kv = [dot(n, w_refs[h][...], ((1,), (0,))).astype(BF) for h in heads]
    scores = [
        dot(q_ref[:, h * DH : (h + 1) * DH], kv[h][:, :DH], ((1,), (1,))) * inv_root for h in heads
    ]
    weights = [jnp.exp(s - jnp.max(s, axis=-1, keepdims=True)) for s in scores]
    probs = [w / jnp.sum(w, axis=-1, keepdims=True) for w in weights]
    ctx = [dot(probs[h].astype(BF), kv[h][:, DH:], ((1,), (0,))).astype(BF) for h in heads]
    for h in heads:
        kv_ref[:, 2 * h * DH : 2 * (h + 1) * DH] = kv[h]
        probs_ref[0, h] = probs[h]
        place = lax.rem(place_ref[0] + h, HEADS) * DH
        ctx_ref[:, pl.ds(pl.multiple_of(place, DH), DH)] = ctx[h]


def backward_kernel(place_ref, q_ref, g_ref, kv_ref, probs_ref, dq_ref, early_ref, late_ref, dkv_ref):
    heads = range(HEADS)
    inv_root = 1.0 / math.sqrt(DH)
    q = [q_ref[:, h * DH : (h + 1) * DH] for h in heads]
    g = [g_ref[:, h * DH : (h + 1) * DH] for h in heads]
    k = [kv_ref[:, 2 * h * DH : (2 * h + 1) * DH] for h in heads]
    v = [kv_ref[:, (2 * h + 1) * DH : 2 * (h + 1) * DH] for h in heads]
    probs = [probs_ref[0, h] for h in heads]
    grad_probs = [dot(g[h], v[h], ((1,), (1,))) for h in heads]
    row_dot = [jnp.sum(grad_probs[h] * probs[h], axis=-1, keepdims=True) for h in heads]
    grad_scores = [
        (probs[h] * (grad_probs[h] - row_dot[h]) * inv_root).astype(BF) for h in heads
    ]
    dv = [dot(probs[h].astype(BF), g[h], ((0,), (0,))).astype(BF) for h in heads]
    dq = [dot(grad_scores[h], k[h], ((1,), (0,))).astype(BF) for h in heads]
    dk = [dot(grad_scores[h], q[h], ((0,), (0,))).astype(BF) for h in heads]
    for h in heads:
        dq_ref[:, h * DH : (h + 1) * DH] = dq[h]
        place = pl.multiple_of(lax.rem(place_ref[0] + h, HEADS) * DH, DH)
        dkv_ref[:, pl.ds(pl.multiple_of(2 * place, DH), DH)] = dk[h]
        dkv_ref[:, pl.ds(pl.multiple_of(2 * place + DH, DH), DH)] = dv[h]
    for i in range(2):
        early_ref[:, i * DH : (i + 1) * DH] = dq[EARLY[i]]
        late_ref[:, i * DH : (i + 1) * DH] = dq[LATE[i]]


def over_stretches(kernel, operands, others, out_shapes, flops, transcendentals=0):
    others = jax.tree.leaves(others)
    count = operands[0].shape[0] // STRETCH

    def spec(array):
        block = (array.shape[0] // count,) + array.shape[1:]
        return pl.BlockSpec(block, lambda i, _: (i,) + (0,) * (len(block) - 1))

    flat, specs = [], []
    for operand in operands:
        if isinstance(operand, list):
            flat += operand
            specs += [pl.BlockSpec(array.shape, lambda i, _: (0, 0)) for array in operand]
        else:
            flat.append(operand)
            specs.append(spec(operand))
    arrays = flat + out_shapes
    return pl.pallas_call(
        kernel,
        grid_spec=pltpu.PrefetchScalarGridSpec(
            num_scalar_prefetch=1,
            grid=(count,),
            in_specs=specs + [pl.BlockSpec(memory_space=pl.ANY)] * len(others),
            out_specs=[spec(array) for array in out_shapes],
        ),
        out_shape=out_shapes,
        compiler_params=pltpu.CompilerParams(vmem_limit_bytes=40 * 1024 * 1024),
        cost_estimate=pl.CostEstimate(
            flops=flops,
            bytes_accessed=sum(array.size * array.dtype.itemsize for array in arrays),
            transcendentals=transcendentals,
        ),
    )(lax.axis_index("y").reshape(1), *flat, *others)


def forward(q, n_rows, w_pairs, *others):
    rows, cols = q.shape
    out_shapes = [
        jax.ShapeDtypeStruct((n_rows.shape[0], 2 * cols), BF),
        jax.ShapeDtypeStruct((rows // STRETCH, HEADS, STRETCH, SPAN), jnp.float32),
        jax.ShapeDtypeStruct(q.shape, BF),
    ]
    flops = 4 * rows * SPAN * cols + 4 * n_rows.size * cols
    return over_stretches(
        forward_kernel, [q, n_rows, w_pairs], others, out_shapes, flops, rows * SPAN * HEADS
    )


def backward(q, g, kv, probs):
    out_shapes = [
        jax.ShapeDtypeStruct(q.shape, BF),
        jax.ShapeDtypeStruct((q.shape[0], 2 * DH), BF),
        jax.ShapeDtypeStruct((q.shape[0], 2 * DH), BF),
        jax.ShapeDtypeStruct(kv.shape, BF),
    ]
    flops = 8 * q.shape[0] * SPAN * q.shape[1]
    return over_stretches(backward_kernel, [q, g, kv, probs], [], out_shapes, flops)


def hop(array, axis, step):
    n = lax.axis_size(axis)
    return lax.ppermute(array, axis, [(i, (i + step) % n) for i in range(n)])


def idle_kernel(*refs):
    del refs


def after(arrays, *others):
    flat, tree = jax.tree.flatten(arrays)
    operands = flat + jax.tree.leaves(others)
    anywhere = pl.BlockSpec(memory_space=pl.ANY)
    kept = pl.pallas_call(
        idle_kernel,
        in_specs=[anywhere] * len(operands),
        out_specs=[anywhere] * len(flat),
        out_shape=[jax.ShapeDtypeStruct(array.shape, array.dtype) for array in flat],
        input_output_aliases={i: i for i in range(len(flat))},
        cost_estimate=pl.CostEstimate(flops=0, bytes_accessed=0, transcendentals=0),
    )(*operands)
    return jax.tree.unflatten(tree, kept)


def near(block, axis):
    return hop(block, axis, -1), hop(block, axis, 1)


def far(later, before, axis):
    half = later.shape[0] // 2
    return jnp.concatenate([hop(later[:half], axis, -1), hop(before[half:], axis, 1)], 0)


def gather_ring(block, axis):
    later, before = near(block, axis)
    return [block, later, far(later, before, axis), before]


def reduce_ring(parts, axis):
    own, later, opposite, before = parts
    half = opposite.shape[0] // 2
    low = hop(opposite[:half], axis, 1)
    high = hop(opposite[half:], axis, -1)
    later = jnp.concatenate([later[:half] + low, later[half:]], 0)
    before = jnp.concatenate([before[:half], before[half:] + high], 0)
    f32 = jnp.float32
    total = own.astype(f32) + hop(later, axis, 1).astype(f32) + hop(before, axis, -1).astype(f32)
    return total.astype(BF)


def sum_kernel(in_ref, *out_refs):
    total = jnp.sum(in_ref[...].astype(jnp.float32), 0).astype(BF)
    for i in range(2):
        out_refs[i][...] = total[:, i * DH : (i + 1) * DH]


def sum_pair(array):
    n = lax.axis_size("z")
    terms = lax.all_to_all(array, "z", split_axis=0, concat_axis=0, tiled=True)
    rows, cols = array.shape[0] // n, array.shape[1]
    size = rows // 4
    return pl.pallas_call(
        sum_kernel,
        grid=(4,),
        in_specs=[pl.BlockSpec((n, size, cols), lambda i: (0, i, 0))],
        out_specs=[pl.BlockSpec((size, DH), lambda i: (i, 0))] * 2,
        out_shape=[jax.ShapeDtypeStruct((rows, DH), BF)] * 2,
        cost_estimate=pl.CostEstimate(
            flops=array.size, bytes_accessed=2 * array.size, transcendentals=0
        ),
    )(terms.reshape(n, rows, cols))


def sum_parts(array, axis):
    terms = lax.all_to_all(array, axis, split_axis=0, concat_axis=0, tiled=True)
    terms = terms.reshape((lax.axis_size(axis), -1) + array.shape[1:]).astype(jnp.float32)
    return jnp.sum(terms, 0).astype(BF)


def z_gather(block):
    n = lax.axis_size("z")
    blocks = gather_ring(block, "z")
    size = block.shape[0]
    start = lax.rem(n - lax.axis_index("z"), n) * size
    twice = jnp.concatenate(blocks + blocks[:-1], 0)
    return lax.dynamic_slice_in_dim(twice, start, n * size, 0).astype(jnp.float32)


def z_spread(block):
    n = lax.axis_size("z")
    copies = jnp.broadcast_to(block[None], (n,) + block.shape).reshape((-1,) + block.shape[1:])
    blocks = lax.all_to_all(copies, "z", split_axis=0, concat_axis=0, tiled=True)
    return blocks.astype(jnp.float32)


def shift(block):
    n = lax.axis_size(SEQ)
    later = lax.ppermute(block, SEQ, [(i, i - 1) for i in range(1, n)])
    return jnp.concatenate([block[STRETCH - 1 :], later[: STRETCH - 1]], 0)


def unshift(block):
    n = lax.axis_size(SEQ)
    earlier = lax.ppermute(block, SEQ, [(i, i + 1) for i in range(n - 1)])
    return jnp.concatenate([earlier[1:], block[:1]], 0)


def copy_kernel(ids_ref, in_ref, *refs):
    refs[-1][...] = in_ref[...]


def pick(units, ids, *others):
    others = jax.tree.leaves(others)
    block = (1,) + units.shape[1:]
    return pl.pallas_call(
        copy_kernel,
        grid_spec=pltpu.PrefetchScalarGridSpec(
            num_scalar_prefetch=1,
            grid=ids.shape,
            in_specs=[pl.BlockSpec(block, lambda i, ids_ref: (ids_ref[i], 0, 0))]
            + [pl.BlockSpec(memory_space=pl.ANY)] * len(others),
            out_specs=pl.BlockSpec(block, lambda i, ids_ref: (i, 0, 0)),
        ),
        out_shape=jax.ShapeDtypeStruct(ids.shape + units.shape[1:], units.dtype),
        cost_estimate=pl.CostEstimate(
            flops=0, bytes_accessed=4 * ids.size * units[0].size, transcendentals=0
        ),
    )(ids, units, *others)


def shards(tokens, grad_in, enc_store, nbr_owner, nbr_row, w_query, w_key, w_value, w_out):
    w_pair = jnp.concatenate([w_key, w_value], 1)
    first = lax.axis_index(SEQ) * NBRS
    owners = lax.dynamic_slice_in_dim(nbr_owner, first, NBRS, 1)
    rows = lax.dynamic_slice_in_dim(nbr_row, first, NBRS, 1)
    own = lax.dynamic_index_in_dim(owners, lax.axis_index("z"), 0, keepdims=False)
    from_units = own * NBRS + jnp.arange(NBRS, dtype=jnp.int32)

    t_own = shift(tokens)
    q_near = near(w_query, "y")
    t_rows = lax.all_gather(t_own, ROWS, axis=0, tiled=True)
    g_own = shift(grad_in)
    outgoing = pick(enc_store, rows.reshape(-1), t_own)
    arrived = lax.all_to_all(outgoing, "z", split_axis=0, concat_axis=0, tiled=True)
    units = pick(arrived, from_units, t_rows, q_near, g_own)
    n_rows = lax.all_gather(units, ROWS, axis=0, tiled=True).reshape(-1, ENC)
    pair_near = near(w_pair, "y")
    q_far = far(*q_near, "y")
    pair_far = far(*pair_near, "y")
    out_near = near(after(w_out, q_near), "y")
    g_own = after(g_own, n_rows, q_far, out_near)
    g_rows = lax.all_gather(g_own, ROWS, axis=0, tiled=True)
    wq = jnp.concatenate([w_query, q_near[0], q_far, q_near[1]], 1)
    q = dot(t_rows, wq, ((1,), (0,))).astype(BF)
    w_pairs = [w_pair, pair_near[0], pair_far, pair_near[1]]
    kv, probs, ctx = forward(q, n_rows, w_pairs)
    half = w_out.shape[0] // 2
    out_far = [hop(out_near[0][:half], "y", -1), hop(out_near[1][half:], "y", 1)]
    d_out = dot(after(ctx, out_far), g_rows, ((0,), (0,))).astype(BF)
    wo = jnp.concatenate([w_out, out_near[0], *out_far, out_near[1]], 0)
    g = dot(g_rows, after(wo, d_out), ((1,), (1,))).astype(BF)
    dq, early, late, dkv = backward(q, g, kv, probs)
    early = dot(t_rows, early, ((0,), (0,))).astype(BF)
    term = dot(after(dq, early), wq, ((1,), (1,))).astype(BF)
    d_pair = dot(after(dkv, term), n_rows, ((0,), (0,))).astype(BF)
    early = sum_pair(early)
    late = sum_pair(after(dot(t_rows, late, ((0,), (0,))).astype(BF), early, d_pair))

    d_out = lax.psum_scatter(d_out, "y", scatter_dimension=0, tiled=True)
    d_pair = lax.psum_scatter(after(d_pair, d_out, early), "y", scatter_dimension=0, tiled=True)
    late = after(late, d_pair)
    term = lax.psum_scatter(after(term, d_pair), ROWS, scatter_dimension=0, tiled=True)
    d_query = reduce_ring([late[1], early[1], early[0], late[0]], "y")
    width = d_out.shape[1]
    d_pair = d_pair.reshape(4, -1, 2, ENC)
    rest = jnp.concatenate([d_out.reshape(4, -1, width), d_pair[:, :, 0], d_pair[:, :, 1]], 2)
    rest = sum_parts(after(rest, late).reshape(DH, -1), "z")
    d_query = z_gather(after(d_query, rest))
    rest = z_gather(rest)
    d_out = rest[:, :width]
    d_pair = jnp.stack([rest[:, width : width + ENC], rest[:, width + ENC :]], 1)
    d_pair = d_pair.reshape(2 * DH, ENC).T
    grad_tokens = unshift(term)
    return grad_tokens, d_query, d_pair[:, :DH], d_pair[:, DH:], d_out


def solution(mesh):
    devices = mesh.devices.reshape(4, 4, 4, 2)
    torus = Mesh(devices, ("z", "x", "y", "c"))
    rows = P(("z", "x", "y", "c"))
    cols = P(None, SEQ)
    in_specs = (rows, rows, rows, P(), P(), cols, cols, cols, P(SEQ))
    out_specs = (rows, cols, cols, cols, P(SEQ))
    return jax.shard_map(shards, mesh=torus, in_specs=in_specs, out_specs=out_specs, check_vma=False)
```

time: 599 us -> 328 us (0.55)
  waiting for transfers between devices: 428 us -> 125 us
  matrix products: 115 us -> 40.5 us
  starting transfers between devices: 5.68 us -> 65.3 us
  Pallas kernels: 0 us -> 29.6 us
  local copies, waits for them, and re-layouts: 27.5 us -> 38 us
  other arithmetic: 2.83 us -> 8.92 us
    all_gather x3, waiting for transfers between devices: 190 us -> 0.04 us  [the longest x1 0.02 us: shards(): n_rows = lax.all_gather(units, ROWS, axis=0, tiled=True).reshape(-1, ENC)]
    reduce_scatter x1 -> x3, waiting for transfers between devices: 114 us -> 0.01 us  [the longest x1 0.01 us: shards(): d_out = lax.psum_scatter(d_out, 'y', scatter_dimension=0, tiled=True)]
    psum x1 -> x0, waiting for transfers between devices: 99.6 us -> none  [shards(): lax.psum((query_part, pair_part, out_sum), 'dp')]
    ppermute x0 -> x27, waiting for transfers between devices: none -> 92.8 us  [the longest x24 64.9 us: hop(): return lax.ppermute(array, axis, [(i, (i + step) % n) for i in range(n)])]
    dot_general x15 -> x7, matrix products: 115 us -> 40.5 us  [dot(): lax.dot_general(left, right, (dims, ((), ())), preferred_element_type=jnp...]
    ppermute x0 -> x27, starting transfers between devices: none -> 46.9 us  [the longest x24 36.6 us: hop(): return lax.ppermute(array, axis, [(i, (i + step) % n) for i in range(n)])]
    pallas_call x0 -> x18, Pallas kernels: none -> 29.6 us  [the longest x2 14.2 us: over_stretches(): pl.pallas_call(kernel, grid_spec=pltpu.PrefetchScalarGridSpec(num_scalar_...]
    unnamed x30 -> x88, local copies, waits for them, and re-layouts: 7.11 us -> 24.4 us
  transfers between devices with their start and end apart: 6 -> 37, of which waited for: 6 -> 18; matrix products, arithmetic and copies ran while one was open for 6% -> 21% of each run, Pallas kernels for 0% -> 8%
where the time goes in v1:
time: 328 us; the launch traced here: 322 us
  waiting for transfers between devices  125 us (38%)
  starting transfers between devices  65.3 us (20%)
  matrix products  40.5 us (12%)
  local copies, waits for them, and re-layouts  38 us (12%)
  Pallas kernels  29.6 us (9%)
  between operations  14.9 us (5%)
  other arithmetic  8.92 us (3%)
    ppermute x24, waiting for transfers between devices, hop(): return lax.ppermute(array, axis, [(i, (i + step) % n) for i in range(n)])  64.9 us
    dot_general x7, matrix products, dot(): lax.dot_general(left, right, (dims, ((), ())), preferred_element_type=jnp...  40.5 us
    ppermute x24, starting transfers between devices, hop(): return lax.ppermute(array, axis, [(i, (i + step) % n) for i in range(n)])  36.6 us
    unnamed x88, local copies, waits for them, and re-layouts  24.4 us
    all_to_all x2, waiting for transfers between devices, sum_pair(): terms = lax.all_to_all(array, 'z', split_axis=0, concat_axis=0, tiled=True)  24 us
    ppermute x2, waiting for transfers between devices, shift(): later = lax.ppermute(block, SEQ, [(i, i - 1) for i in range(1, n)])  21.3 us
    pallas_call x2, Pallas kernels, over_stretches(): pl.pallas_call(kernel, grid_spec=pltpu.PrefetchScalarGridSpec(num_scalar_...  14.2 us
    all_to_all x2, starting transfers between devices, sum_pair(): terms = lax.all_to_all(array, 'z', split_axis=0, concat_axis=0, tiled=True)  9.26 us
  transfers between devices with their start and end apart: 37, of which 18 were waited for; matrix products, arithmetic and copies ran while one was open for 21% of the time, Pallas kernels for 8%

profile of v1, /device:TPU:2, one launch (start us, length us, event | category | flops | bytes accessed | tf_op | source)
XLA Modules:
  0.0 322.3 jit_solution(1280061868613049282)
XLA Ops:
  8.5 4.3 %collective-permute-start = (bf16[64,4096]{1,0:T(8,128)(2,1)}, bf16[64,4096]{1,0:T(8,128)(2,1)S(1)}, u32[]{:S(2)}, u32[]{:S(2)}) collective-permute-start(bf16[64,4096]{1,0:T(8,128)(2,1)} %param.9), channel_id=1, source_target_pairs={{1,0},{2,1},{3,2},{4,3},{5,4},{6,5},{7,6},{8,7},{9,8},{10,9},{11,1... | collective-permute-start | bytes 1572872 | tf_op jit(solution)/shard_map/ppermute | solution.py:228
  13.7 6.1 %collective-permute-done = bf16[64,4096]{1,0:T(8,128)(2,1)S(1)} collective-permute-done((bf16[64,4096]{1,0:T(8,128)(2,1)}, bf16[64,4096]{1,0:T(8,128)(2,1)S(1)}, u32[]{:S(2)}, u32[]{:S(2)}) %collective-permute-start) | collective-permute-done | bytes 524320 | tf_op jit(solution)/shard_map/ppermute | solution.py:228
  21.4 5.9 %shard_map.128 = bf16[8,128,896]{2,1,0:T(8,128)(2,1)} custom-call(s32[8]{0:T(128)} %reshape.46.ids_ref, bf16[4,128,896]{2,1,0:T(8,128)(2,1)} %in_ref.1, bf16[64,4096]{1,0:T(8,128)(2,1)} %pad_maximum_fusion.5.refs_0_), custom_call_target="tpu_custom_call" | custom-call | bytes 3670016 | tf_op jit(solution)/shard_map/pallas_call | solution.py:245
  27.3 5.3 %all-to-all-start = ((bf16[8,128,896]{2,1,0:T(8,128)(2,1)}), bf16[8,128,896]{2,1,0:T(8,128)(2,1)S(1)}, u32[]{:S(2)}, u32[]{:S(2)}) async-start(bf16[8,128,896]{2,1,0:T(8,128)(2,1)} %shard_map.128), calls=%async_computation | async-start | bytes 3670016 | tf_op jit(solution)/shard_map/all_to_all | solution.py:274
  35.9 4.1 %collective-permute-start.5 = (bf16[64,4096]{1,0:T(8,128)(2,1)}, bf16[64,4096]{1,0:T(8,128)(2,1)S(1)}, u32[]{:S(2)}, u32[]{:S(2)}) collective-permute-start(bf16[64,4096]{1,0:T(8,128)(2,1)} %param.10), channel_id=1, source_target_pairs={{1,0},{2,1},{3,2},{4,3},{5,4},{6,5},{7,6},{8,7},{9,8},{10,9},{11,1... | collective-permute-start | bytes 1572872 | tf_op jit(solution)/shard_map/ppermute | solution.py:228
  42.1 15.2 %collective-permute-done.5 = bf16[64,4096]{1,0:T(8,128)(2,1)S(1)} collective-permute-done((bf16[64,4096]{1,0:T(8,128)(2,1)}, bf16[64,4096]{1,0:T(8,128)(2,1)S(1)}, u32[]{:S(2)}, u32[]{:S(2)}) %collective-permute-start.5) | collective-permute-done | bytes 524320 | tf_op jit(solution)/shard_map/ppermute | solution.py:228
  59.8 5.3 %collective-permute-done.1.refs_1_ = bf16[4096,128]{1,0:T(8,128)(2,1)} collective-permute-done((bf16[4096,128]{1,0:T(8,128)(2,1)}, bf16[4096,128]{1,0:T(8,128)(2,1)}, u32[]{:S(2)}, u32[]{:S(2)}) %collective-permute-start.1) | collective-permute-done | bytes 1048608 | tf_op jit(solution)/shard_map/ppermute | solution.py:133
  69.9 3.7 %collective-permute-start.6 = (bf16[128,4096]{1,0:T(8,128)(2,1)}, bf16[128,4096]{1,0:T(8,128)(2,1)S(1)}, u32[]{:S(2)}, u32[]{:S(2)}) collective-permute-start(bf16[128,4096]{1,0:T(8,128)(2,1)} %shard_map.130), channel_id=1, source_target_pairs={{0,6},{2,0},{4,2},{6,4},{1,7},{3,1},{5,3},{7,5},{8,14},{10,8},{12,... | collective-permute-start | bytes 3145736 | tf_op jit(solution)/shard_map/ppermute | solution.py:133
  79.1 28.6 %collective-permute-done.2 = bf16[2048,128]{1,0:T(8,128)(2,1)S(1)} collective-permute-done((bf16[2048,128]{1,0:T(8,128)(2,1)S(1)}, bf16[2048,128]{1,0:T(8,128)(2,1)S(1)}, u32[]{:S(2)}, u32[]{:S(2)}) %collective-permute-start.2) | collective-permute-done | bytes 524320 | tf_op jit(solution)/shard_map/ppermute | solution.py:133
  107.8 3.4 %collective-permute-done.4 = bf16[2048,128]{1,0:T(8,128)(2,1)S(1)} collective-permute-done((bf16[2048,128]{1,0:T(8,128)(2,1)S(1)}, bf16[2048,128]{1,0:T(8,128)(2,1)S(1)}, u32[]{:S(2)}, u32[]{:S(2)}) %collective-permute-start.4) | collective-permute-done | bytes 524320 | tf_op jit(solution)/shard_map/ppermute | solution.py:133
  118.4 9.4 %collective-permute-done.12.refs_3_ = bf16[896,256]{1,0:T(8,128)(2,1)S(1)} collective-permute-done((bf16[896,256]{1,0:T(8,128)(2,1)S(1)}, bf16[896,256]{1,0:T(8,128)(2,1)S(1)}, u32[]{:S(2)}, u32[]{:S(2)}) %collective-permute-start.12) | collective-permute-done | bytes 458784 | tf_op jit(solution)/shard_map/ppermute | solution.py:133
  131.1 3.9 %collective-permute-done.13 = bf16[448,256]{1,0:T(8,128)(2,1)S(1)} collective-permute-done((bf16[448,256]{1,0:T(8,128)(2,1)S(1)}, bf16[448,256]{1,0:T(8,128)(2,1)S(1)}, u32[]{:S(2)}, u32[]{:S(2)}) %collective-permute-start.13) | collective-permute-done | bytes 229408 | tf_op jit(solution)/shard_map/ppermute | solution.py:133
  135.1 3.4 %collective-permute-start.8 = (bf16[64,4096]{1,0:T(8,128)(2,1)S(1)}, bf16[64,4096]{1,0:T(8,128)(2,1)}, u32[]{:S(2)}, u32[]{:S(2)}) collective-permute-start(bf16[64,4096]{1,0:T(8,128)(2,1)S(1)} %slice.120), channel_id=1, source_target_pairs={{0,6},{2,0},{4,2},{6,4},{1,7},{3,1},{5,3},{7,5},{8,14},{10,8},{12,... | collective-permute-start | bytes 1572872 | tf_op jit(solution)/shard_map/ppermute | solution.py:133
  138.9 5.4 %convolution_convert_fusion.6.q_ref = bf16[512,512]{1,0:T(8,128)(2,1)S(1)} fusion(bf16[512,4096]{1,0:T(8,128)(2,1)} %all-gather.4.cloned.1.call-done.refs_0_, bf16[4096,128]{1,0:T(8,128)(2,1)} %collective-permute-done.3.refs_2_, bf16[4096,128]{1,0:T(8,128)(2,1)S(1)} %copy-done.24, bf16[4096,128]{1,0:T(8,128)(2,1)} %collective-permute-done.1.refs_1_, ...), kind=kOutput, calls=%fused_computation.9 | convolution fusion | flops 2164523008 | bytes 8912896 | tf_op jit(solution)/shard_map/dot_general | solution.py:24
  144.2 9.3 %shard_map.132 = (bf16[2048,1024]{1,0:T(8,128)(2,1)S(1)}, f32[8,4,64,256]{3,2,1,0:T(8,128)S(1)}, bf16[512,512]{1,0:T(8,128)(2,1)S(1)}) custom-call(s32[1]{0:T(128)} %bitcast.place_ref, bf16[512,512]{1,0:T(8,128)(2,1)S(1)} %convolution_convert_fusion.6.q_ref, bf16[2048,896]{1,0:T(8,128)(2,1)S(1)} %bitcast.32, ...), custom_call_target="tpu_custom_call" | custom-call | flops 4026531840 | bytes 12845056 | tf_op jit(solution)/shard_map/pallas_call | solution.py:89
  156.3 6.8 %convolution_convert_fusion.1.refs_1_ = bf16[512,4096]{1,0:T(8,128)(2,1)} fusion(bf16[512,512]{1,0:T(8,128)(2,1)} %shard_map.133, bf16[512,4096]{1,0:T(8,128)(2,1)} %all-gather.8.cloned.1.call-done), kind=kOutput, calls=%fused_computation.1 | convolution fusion | flops 2149580800 | bytes 8912896 | tf_op jit(solution)/shard_map/dot_general | solution.py:24
  170.3 6.0 %convolution_convert_fusion.5.g_ref = bf16[512,512]{1,0:T(8,128)(2,1)S(1)} fusion(bf16[512,4096]{1,0:T(8,128)(2,1)} %all-gather.8.cloned.1.call-done, bf16[512,4096]{1,0:T(8,128)(2,1)} %shard_map.134), kind=kOutput, calls=%fused_computation.8 | convolution fusion | flops 2147745792 | bytes 8912896 | tf_op jit(solution)/shard_map/dot_general | solution.py:24
  176.3 4.9 %shard_map.135 = (bf16[512,512]{1,0:T(8,128)(2,1)S(1)}, bf16[512,256]{1,0:T(8,128)(2,1)S(1)}, bf16[512,256]{1,0:T(8,128)(2,1)S(1)}, bf16[2048,1024]{1,0:T(8,128)(2,1)S(1)}) custom-call(s32[1]{0:T(128)} %bitcast.place_ref, bf16[512,512]{1,0:T(8,128)(2,1)S(1)} %convolution_convert_fusion.6.q_ref, bf16[512,512]{1,0:T(8,128)(2,1)S(1)} %convolution_convert_fusion.5.g_ref, ...), custom_call_target="tpu_custom_call" | custom-call | flops 536870912 | bytes 12582912 | tf_op jit(solution)/shard_map/pallas_call | solution.py:89
  184.1 5.5 %all-to-all-start.1 = ((bf16[4,1024,256]{2,1,0:T(8,128)(2,1)}), bf16[4,1024,256]{2,1,0:T(8,128)(2,1)S(1)}, u32[]{:S(2)}, u32[]{:S(2)}) async-start(bf16[4,1024,256]{2,1,0:T(8,128)(2,1)} %bitcast.34), calls=%async_computation.2 | async-start | bytes 4194304 | tf_op jit(solution)/shard_map/all_to_all | solution.py:189
  189.6 6.7 %convolution_convert_fusion.refs_1_.refs_0_ = bf16[512,4096]{1,0:T(8,128)(2,1)} fusion(bf16[512,512]{1,0:T(8,128)(2,1)S(1)} %copy-done.8, bf16[4096,128]{1,0:T(8,128)(2,1)} %collective-permute-done.3.refs_2_, bf16[4096,128]{1,0:T(8,128)(2,1)} %copy-done.23, bf16[4096,128]{1,0:T(8,128)(2,1)} %collective-permute-done.1.refs_1_, bf16[4096,128]{1,0:T(8,128)(2,1)} %param.14), kind=kOutput, calls=%fused_computation | convolution fusion | flops 2166358016 | bytes 8912896 | tf_op jit(solution)/shard_map/dot_general | solution.py:24
  196.4 8.0 %convolution_convert_fusion.4.refs_3_ = bf16[1024,896]{1,0:T(8,128)(2,1)S(1)} fusion(bf16[2048,1024]{1,0:T(8,128)(2,1)} %shard_map.137, bf16[2048,896]{1,0:T(8,128)(2,1)} %bitcast.31), kind=kOutput, calls=%fused_computation.5 | convolution fusion | flops 3759013888 | bytes 9699328 | tf_op jit(solution)/shard_map/dot_general | solution.py:24
  206.8 5.2 %all-to-all-done.1.in_ref = bf16[4,1024,256]{2,1,0:T(8,128)(2,1)S(1)} async-done(((bf16[4,1024,256]{2,1,0:T(8,128)(2,1)}), bf16[4,1024,256]{2,1,0:T(8,128)(2,1)S(1)}, u32[]{:S(2)}, u32[]{:S(2)}) %all-to-all-start.1) | async-done | bytes 2097184 | tf_op jit(solution)/shard_map/all_to_all | solution.py:189
  213.3 3.5 %shard_map.138 = (bf16[1024,128]{1,0:T(8,128)(2,1)}, bf16[1024,128]{1,0:T(8,128)(2,1)}) custom-call(bf16[4,1024,256]{2,1,0:T(8,128)(2,1)} %copy-done.10), custom_call_target="tpu_custom_call" | custom-call | flops 1048576 | bytes 2097152 | tf_op jit(solution)/shard_map/pallas_call | solution.py:192
  216.8 4.8 %convolution_convert_fusion.2.refs_0_ = bf16[4096,256]{1,0:T(8,128)(2,1)} fusion(bf16[512,4096]{1,0:T(8,128)(2,1)} %all-gather.4.cloned.1.call-done.refs_0_, bf16[512,256]{1,0:T(8,128)(2,1)S(1)} %get-tuple-element.26), kind=kOutput, calls=%fused_computation.2 | convolution fusion | flops 1074790400 | bytes 6553600 | tf_op jit(solution)/shard_map/dot_general | solution.py:24
  221.7 3.8 %all-to-all-start.2 = ((bf16[4,1024,256]{2,1,0:T(8,128)(2,1)}), bf16[4,1024,256]{2,1,0:T(8,128)(2,1)S(1)}, u32[]{:S(2)}, u32[]{:S(2)}) async-start(bf16[4,1024,256]{2,1,0:T(8,128)(2,1)} %bitcast.33), calls=%async_computation.5 | async-start | bytes 4194304 | tf_op jit(solution)/shard_map/all_to_all | solution.py:189
  228.9 18.9 %all-to-all-done.2.in_ref = bf16[4,1024,256]{2,1,0:T(8,128)(2,1)S(1)} async-done(((bf16[4,1024,256]{2,1,0:T(8,128)(2,1)}), bf16[4,1024,256]{2,1,0:T(8,128)(2,1)S(1)}, u32[]{:S(2)}, u32[]{:S(2)}) %all-to-all-start.2) | async-done | bytes 2097184 | tf_op jit(solution)/shard_map/all_to_all | solution.py:189
  249.0 3.5 %shard_map.142 = (bf16[1024,128]{1,0:T(8,128)(2,1)}, bf16[1024,128]{1,0:T(8,128)(2,1)}) custom-call(bf16[4,1024,256]{2,1,0:T(8,128)(2,1)} %copy-done.11), custom_call_target="tpu_custom_call" | custom-call | flops 1048576 | bytes 2097152 | tf_op jit(solution)/shard_map/pallas_call | solution.py:192
  255.7 3.7 %all-to-all-start.3 = ((bf16[4,32,5888]{2,1,0:T(8,128)(2,1)}), bf16[4,32,5888]{2,1,0:T(8,128)(2,1)S(1)}, u32[]{:S(2)}, u32[]{:S(2)}) async-start(bf16[4,32,5888]{2,1,0:T(8,128)(2,1)} %shard_map.144), calls=%async_computation.6 | async-start | bytes 3014656 | tf_op jit(solution)/shard_map/all_to_all | solution.py:205
  263.0 4.2 %collective-permute-done.16 = bf16[1024,128]{1,0:T(8,128)(2,1)S(1)} collective-permute-done((bf16[1024,128]{1,0:T(8,128)(2,1)S(1)}, bf16[1024,128]{1,0:T(8,128)(2,1)S(1)}, u32[]{:S(2)}, u32[]{:S(2)}) %collective-permute-start.16) | collective-permute-done | bytes 262176 | tf_op jit(solution)/shard_map/ppermute | solution.py:133
  268.0 8.2 %all-to-all-done.3 = bf16[4,32,5888]{2,1,0:T(8,128)(2,1)S(1)} async-done(((bf16[4,32,5888]{2,1,0:T(8,128)(2,1)}), bf16[4,32,5888]{2,1,0:T(8,128)(2,1)S(1)}, u32[]{:S(2)}, u32[]{:S(2)}) %all-to-all-start.3) | async-done | bytes 1507360 | tf_op jit(solution)/shard_map/all_to_all | solution.py:205
  296.0 3.7 %collective-permute-done.26 = bf16[16,5888]{1,0:T(8,128)(2,1)S(1)} collective-permute-done((bf16[16,5888]{1,0:T(8,128)(2,1)S(1)}, bf16[16,5888]{1,0:T(8,128)(2,1)S(1)}, u32[]{:S(2)}, u32[]{:S(2)}) %collective-permute-start.26) | collective-permute-done | bytes 188448 | tf_op jit(solution)/shard_map/ppermute | solution.py:133
  307.9 6.5 %collective-permute-done.14 = bf16[64,4096]{1,0:T(8,128)(2,1)S(1)} collective-permute-done((bf16[64,4096]{1,0:T(8,128)(2,1)}, bf16[64,4096]{1,0:T(8,128)(2,1)S(1)}, u32[]{:S(2)}, u32[]{:S(2)}) %collective-permute-start.14) | collective-permute-done | bytes 524320 | tf_op jit(solution)/shard_map/ppermute | solution.py:234
  (206 shorter events, 90.4 us)
Async XLA Ops:
  7.2 57.9 %all-gather.4.cloned.1.call-start = ((), (), s32[]{:S(2)}) async-start(), calls=%async_computation.7 | async-start | bytes 4718592 | tf_op jit(solution)/shard_map/all_gather | solution.py:271
  8.5 11.3 %collective-permute-start = (bf16[64,4096]{1,0:T(8,128)(2,1)}, bf16[64,4096]{1,0:T(8,128)(2,1)S(1)}, u32[]{:S(2)}, u32[]{:S(2)}) collective-permute-start(bf16[64,4096]{1,0:T(8,128)(2,1)} %param.9), channel_id=1, source_target_pairs={{1,0},{2,1},{3,2},{4,3},{5,4},{6,5},{7,6},{8,7},{9,8},{10,9},{11,1... | collective-permute-start | bytes 1572872 | tf_op jit(solution)/shard_map/ppermute | solution.py:228
  27.3 37.7 %all-to-all-start = ((bf16[8,128,896]{2,1,0:T(8,128)(2,1)}), bf16[8,128,896]{2,1,0:T(8,128)(2,1)S(1)}, u32[]{:S(2)}, u32[]{:S(2)}) async-start(bf16[8,128,896]{2,1,0:T(8,128)(2,1)} %shard_map.128), calls=%async_computation | async-start | bytes 3670016 | tf_op jit(solution)/shard_map/all_to_all | solution.py:274
  32.6 78.6 %all-gather.6.cloned.1.call-start = ((), (), s32[]{:S(2)}) async-start(), calls=%async_computation.8 | async-start | bytes 4128768 | tf_op jit(solution)/shard_map/all_gather | solution.py:276
  32.7 27.1 %collective-permute-start.3 = (bf16[4096,128]{1,0:T(8,128)(2,1)}, bf16[4096,128]{1,0:T(8,128)(2,1)}, u32[]{:S(2)}, u32[]{:S(2)}) collective-permute-start(bf16[4096,128]{1,0:T(8,128)(2,1)} %param.14), channel_id=1, source_target_pairs={{0,2},{2,4},{4,6},{6,0},{1,3},{3,5},{5,7},{7,1},{8,10},{10,12},{12... | collective-permute-start | bytes 3145736 | tf_op jit(solution)/shard_map/ppermute | solution.py:133
  32.7 32.4 %collective-permute-start.1 = (bf16[4096,128]{1,0:T(8,128)(2,1)}, bf16[4096,128]{1,0:T(8,128)(2,1)}, u32[]{:S(2)}, u32[]{:S(2)}) collective-permute-start(bf16[4096,128]{1,0:T(8,128)(2,1)} %param.14), channel_id=1, source_target_pairs={{0,6},{2,0},{4,2},{6,4},{1,7},{3,1},{5,3},{7,5},{8,14},{10,8},{12,... | collective-permute-start | bytes 3145736 | tf_op jit(solution)/shard_map/ppermute | solution.py:133
  35.9 21.4 %collective-permute-start.5 = (bf16[64,4096]{1,0:T(8,128)(2,1)}, bf16[64,4096]{1,0:T(8,128)(2,1)S(1)}, u32[]{:S(2)}, u32[]{:S(2)}) collective-permute-start(bf16[64,4096]{1,0:T(8,128)(2,1)} %param.10), channel_id=1, source_target_pairs={{1,0},{2,1},{3,2},{4,3},{5,4},{6,5},{7,6},{8,7},{9,8},{10,9},{11,1... | collective-permute-start | bytes 1572872 | tf_op jit(solution)/shard_map/ppermute | solution.py:228
  68.8 87.5 %all-gather.8.cloned.1.call-start = ((), (), s32[]{:S(2)}) async-start(), calls=%async_computation.9 | async-start | bytes 4718592 | tf_op jit(solution)/shard_map/all_gather | solution.py:282
  69.9 41.3 %collective-permute-start.6 = (bf16[128,4096]{1,0:T(8,128)(2,1)}, bf16[128,4096]{1,0:T(8,128)(2,1)S(1)}, u32[]{:S(2)}, u32[]{:S(2)}) collective-permute-start(bf16[128,4096]{1,0:T(8,128)(2,1)} %shard_map.130), channel_id=1, source_target_pairs={{0,6},{2,0},{4,2},{6,4},{1,7},{3,1},{5,3},{7,5},{8,14},{10,8},{12,... | collective-permute-start | bytes 3145736 | tf_op jit(solution)/shard_map/ppermute | solution.py:133
  73.6 37.7 %collective-permute-start.7 = (bf16[128,4096]{1,0:T(8,128)(2,1)}, bf16[128,4096]{1,0:T(8,128)(2,1)S(1)}, u32[]{:S(2)}, u32[]{:S(2)}) collective-permute-start(bf16[128,4096]{1,0:T(8,128)(2,1)} %shard_map.130), channel_id=1, source_target_pairs={{0,2},{2,4},{4,6},{6,0},{1,3},{3,5},{5,7},{7,1},{8,10},{10,12},{12... | collective-permute-start | bytes 3145736 | tf_op jit(solution)/shard_map/ppermute | solution.py:133
  74.7 33.1 %collective-permute-start.2 = (bf16[2048,128]{1,0:T(8,128)(2,1)S(1)}, bf16[2048,128]{1,0:T(8,128)(2,1)S(1)}, u32[]{:S(2)}, u32[]{:S(2)}) collective-permute-start(bf16[2048,128]{1,0:T(8,128)(2,1)S(1)} %slice.117), channel_id=1, source_target_pairs={{0,6},{2,0},{4,2},{6,4},{1,7},{3,1},{5,3},{7,5},{8,14},{10,8},{12,... | collective-permute-start | bytes 1572872 | tf_op jit(solution)/shard_map/ppermute | solution.py:133
  79.0 32.1 %collective-permute-start.4 = (bf16[2048,128]{1,0:T(8,128)(2,1)S(1)}, bf16[2048,128]{1,0:T(8,128)(2,1)S(1)}, u32[]{:S(2)}, u32[]{:S(2)}) collective-permute-start(bf16[2048,128]{1,0:T(8,128)(2,1)S(1)} %slice.118), channel_id=1, source_target_pairs={{0,2},{2,4},{4,6},{6,0},{1,3},{3,5},{5,7},{7,1},{8,10},{10,12},{12... | collective-permute-start | bytes 1572872 | tf_op jit(solution)/shard_map/ppermute | solution.py:133
  113.0 103.8 %reduce-scatter.4.cloned.1.call-start = ((), (), s32[]{:S(2)}) async-start(), calls=%async_computation.10 | async-start | bytes 5242880 | tf_op jit(solution)/shard_map/reduce_scatter | solution.py:299
  115.1 12.7 %collective-permute-start.12 = (bf16[896,256]{1,0:T(8,128)(2,1)S(1)}, bf16[896,256]{1,0:T(8,128)(2,1)S(1)}, u32[]{:S(2)}, u32[]{:S(2)}) collective-permute-start(bf16[896,256]{1,0:T(8,128)(2,1)S(1)} %constant_dynamic-update-slice_fusion.7.refs_0_), channel_id=1, source_target_pairs={{0,2},{2,4},{4,6},{6,0},{1,3},{3,5},{5,7},{7,1},{8,10},{10,12},{12... | collective-permute-start | bytes 1376264 | tf_op jit(solution)/shard_map/ppermute | solution.py:133
  115.1 12.7 %collective-permute-start.10 = (bf16[896,256]{1,0:T(8,128)(2,1)S(1)}, bf16[896,256]{1,0:T(8,128)(2,1)S(1)}, u32[]{:S(2)}, u32[]{:S(2)}) collective-permute-start(bf16[896,256]{1,0:T(8,128)(2,1)S(1)} %constant_dynamic-update-slice_fusion.7.refs_0_), channel_id=1, source_target_pairs={{0,6},{2,0},{4,2},{6,4},{1,7},{3,1},{5,3},{7,5},{8,14},{10,8},{12,... | collective-permute-start | bytes 1376264 | tf_op jit(solution)/shard_map/ppermute | solution.py:133
  127.7 7.3 %collective-permute-start.13 = (bf16[448,256]{1,0:T(8,128)(2,1)S(1)}, bf16[448,256]{1,0:T(8,128)(2,1)S(1)}, u32[]{:S(2)}, u32[]{:S(2)}) collective-permute-start(bf16[448,256]{1,0:T(8,128)(2,1)S(1)} %slice.123), channel_id=1, source_target_pairs={{0,2},{2,4},{4,6},{6,0},{1,3},{3,5},{5,7},{7,1},{8,10},{10,12},{12... | collective-permute-start | bytes 688136 | tf_op jit(solution)/shard_map/ppermute | solution.py:133
  135.1 21.1 %collective-permute-start.8 = (bf16[64,4096]{1,0:T(8,128)(2,1)S(1)}, bf16[64,4096]{1,0:T(8,128)(2,1)}, u32[]{:S(2)}, u32[]{:S(2)}) collective-permute-start(bf16[64,4096]{1,0:T(8,128)(2,1)S(1)} %slice.120), channel_id=1, source_target_pairs={{0,6},{2,0},{4,2},{6,4},{1,7},{3,1},{5,3},{7,5},{8,14},{10,8},{12,... | collective-permute-start | bytes 1572872 | tf_op jit(solution)/shard_map/ppermute | solution.py:133
  138.6 17.7 %collective-permute-start.9 = (bf16[64,4096]{1,0:T(8,128)(2,1)S(1)}, bf16[64,4096]{1,0:T(8,128)(2,1)}, u32[]{:S(2)}, u32[]{:S(2)}) collective-permute-start(bf16[64,4096]{1,0:T(8,128)(2,1)S(1)} %slice.121), channel_id=1, source_target_pairs={{0,2},{2,4},{4,6},{6,0},{1,3},{3,5},{5,7},{7,1},{8,10},{10,12},{12... | collective-permute-start | bytes 1572872 | tf_op jit(solution)/shard_map/ppermute | solution.py:133
  184.1 27.9 %all-to-all-start.1 = ((bf16[4,1024,256]{2,1,0:T(8,128)(2,1)}), bf16[4,1024,256]{2,1,0:T(8,128)(2,1)S(1)}, u32[]{:S(2)}, u32[]{:S(2)}) async-start(bf16[4,1024,256]{2,1,0:T(8,128)(2,1)} %bitcast.34), calls=%async_computation.2 | async-start | bytes 4194304 | tf_op jit(solution)/shard_map/all_to_all | solution.py:189
  189.6 62.9 %reduce-scatter.6.cloned.1.call-start = ((), (), s32[]{:S(2)}) async-start(), calls=%async_computation.11 | async-start | bytes 2293760 | tf_op jit(solution)/shard_map/reduce_scatter | solution.py:300
  221.7 26.1 %all-to-all-start.2 = ((bf16[4,1024,256]{2,1,0:T(8,128)(2,1)}), bf16[4,1024,256]{2,1,0:T(8,128)(2,1)S(1)}, u32[]{:S(2)}, u32[]{:S(2)}) async-start(bf16[4,1024,256]{2,1,0:T(8,128)(2,1)} %bitcast.33), calls=%async_computation.5 | async-start | bytes 4194304 | tf_op jit(solution)/shard_map/all_to_all | solution.py:189
  226.1 33.8 %collective-permute-start.17 = (bf16[512,128]{1,0:T(8,128)(2,1)S(1)}, bf16[512,128]{1,0:T(8,128)(2,1)S(1)}, u32[]{:S(2)}, u32[]{:S(2)}) collective-permute-start(bf16[512,128]{1,0:T(8,128)(2,1)S(1)} %get-tuple-element.50), channel_id=1, source_target_pairs={{0,6},{2,0},{4,2},{6,4},{1,7},{3,1},{5,3},{7,5},{8,14},{10,8},{12,... | collective-permute-start | bytes 393224 | tf_op jit(solution)/shard_map/ppermute | solution.py:133
  228.8 30.6 %collective-permute-start.15 = (bf16[512,128]{1,0:T(8,128)(2,1)}, bf16[512,128]{1,0:T(8,128)(2,1)S(1)}, u32[]{:S(2)}, u32[]{:S(2)}) collective-permute-start(bf16[512,128]{1,0:T(8,128)(2,1)} %get-tuple-element.49), channel_id=1, source_target_pairs={{0,2},{2,4},{4,6},{6,0},{1,3},{3,5},{5,7},{7,1},{8,10},{10,12},{12... | collective-permute-start | bytes 393224 | tf_op jit(solution)/shard_map/ppermute | solution.py:133
  255.7 20.5 %all-to-all-start.3 = ((bf16[4,32,5888]{2,1,0:T(8,128)(2,1)}), bf16[4,32,5888]{2,1,0:T(8,128)(2,1)S(1)}, u32[]{:S(2)}, u32[]{:S(2)}) async-start(bf16[4,32,5888]{2,1,0:T(8,128)(2,1)} %shard_map.144), calls=%async_computation.6 | async-start | bytes 3014656 | tf_op jit(solution)/shard_map/all_to_all | solution.py:205
  259.4 42.2 %reduce-scatter.8.cloned.1.call-start = ((), (), s32[]{:S(2)}) async-start(), calls=%async_computation.12 | async-start | bytes 4718592 | tf_op jit(solution)/shard_map/reduce_scatter | solution.py:302
  259.6 7.7 %collective-permute-start.16 = (bf16[1024,128]{1,0:T(8,128)(2,1)S(1)}, bf16[1024,128]{1,0:T(8,128)(2,1)S(1)}, u32[]{:S(2)}, u32[]{:S(2)}) collective-permute-start(bf16[1024,128]{1,0:T(8,128)(2,1)S(1)} %pad_maximum_fusion.9), channel_id=1, source_target_pairs={{0,2},{2,4},{4,6},{6,0},{1,3},{3,5},{5,7},{7,1},{8,10},{10,12},{12... | collective-permute-start | bytes 786440 | tf_op jit(solution)/shard_map/ppermute | solution.py:133
  277.3 7.5 %collective-permute-start.19 = (bf16[1024,128]{1,0:T(8,128)(2,1)}, bf16[1024,128]{1,0:T(8,128)(2,1)S(1)}, u32[]{:S(2)}, u32[]{:S(2)}) collective-permute-start(bf16[1024,128]{1,0:T(8,128)(2,1)} %shard_map.145), channel_id=1, source_target_pairs={{0,96},{32,0},{64,32},{96,64},{1,97},{33,1},{65,33},{97,65},{2,98}... | collective-permute-start | bytes 786440 | tf_op jit(solution)/shard_map/ppermute | solution.py:133
  277.9 9.4 %collective-permute-start.21 = (bf16[1024,128]{1,0:T(8,128)(2,1)}, bf16[1024,128]{1,0:T(8,128)(2,1)S(1)}, u32[]{:S(2)}, u32[]{:S(2)}) collective-permute-start(bf16[1024,128]{1,0:T(8,128)(2,1)} %shard_map.145), channel_id=1, source_target_pairs={{0,32},{32,64},{64,96},{96,0},{1,33},{33,65},{65,97},{97,1},{2,34}... | collective-permute-start | bytes 786440 | tf_op jit(solution)/shard_map/ppermute | solution.py:133
  279.3 10.8 %collective-permute-start.23 = (bf16[32,5888]{1,0:T(8,128)(2,1)}, bf16[32,5888]{1,0:T(8,128)(2,1)S(1)}, u32[]{:S(2)}, u32[]{:S(2)}) collective-permute-start(bf16[32,5888]{1,0:T(8,128)(2,1)} %reduce_sum.12.refs_1_), channel_id=1, source_target_pairs={{0,96},{32,0},{64,32},{96,64},{1,97},{33,1},{65,33},{97,65},{2,98}... | collective-permute-start | bytes 1130504 | tf_op jit(solution)/shard_map/ppermute | solution.py:133
  281.1 11.8 %collective-permute-start.25 = (bf16[32,5888]{1,0:T(8,128)(2,1)}, bf16[32,5888]{1,0:T(8,128)(2,1)S(1)}, u32[]{:S(2)}, u32[]{:S(2)}) collective-permute-start(bf16[32,5888]{1,0:T(8,128)(2,1)} %reduce_sum.12.refs_1_), channel_id=1, source_target_pairs={{0,32},{32,64},{64,96},{96,0},{1,33},{33,65},{65,97},{97,1},{2,34}... | collective-permute-start | bytes 1130504 | tf_op jit(solution)/shard_map/ppermute | solution.py:133
  284.7 8.3 %collective-permute-start.20 = (bf16[512,128]{1,0:T(8,128)(2,1)S(1)}, bf16[512,128]{1,0:T(8,128)(2,1)S(1)}, u32[]{:S(2)}, u32[]{:S(2)}) collective-permute-start(bf16[512,128]{1,0:T(8,128)(2,1)S(1)} %slice.128), channel_id=1, source_target_pairs={{0,96},{32,0},{64,32},{96,64},{1,97},{33,1},{65,33},{97,65},{2,98}... | collective-permute-start | bytes 393224 | tf_op jit(solution)/shard_map/ppermute | solution.py:133
  301.7 12.8 %collective-permute-start.14 = (bf16[64,4096]{1,0:T(8,128)(2,1)}, bf16[64,4096]{1,0:T(8,128)(2,1)S(1)}, u32[]{:S(2)}, u32[]{:S(2)}) collective-permute-start(bf16[64,4096]{1,0:T(8,128)(2,1)} %reduce-scatter.8.cloned.1.call-done), channel_id=1, source_target_pairs={{0,1},{1,2},{2,3},{3,4},{4,5},{5,6},{6,7},{7,8},{8,9},{9,10},{10,1... | collective-permute-start | bytes 1572872 | tf_op jit(solution)/shard_map/ppermute | solution.py:234
  (36 other events, 328.0 us)
Sparse Core Ops, SparseCore 0:
  20.9 39.4 all-gather.3
  68.9 31.4 all-gather.5
  113.1 30.4 all-gather.7
  163.2 48.6 reduce-scatter.3
  217.0 28.0 reduce-scatter.5
  263.1 33.8 reduce-scatter.7

commit v2 on v1

--- a/solution.py
+++ b/solution.py
@@ -1,3 +1,4 @@
+import functools
 import math
 
 import jax
@@ -16,6 +17,9 @@
 HEADS = 4
 EARLY, LATE = (2, 1), (3, 0)
 BF = jnp.bfloat16
+PARTS = 4
+ANYWHERE = pl.BlockSpec(memory_space=pl.ANY)
+PARAMS = pltpu.CompilerParams(vmem_limit_bytes=40 * 1024 * 1024)
 ROWS = ("x", "c")
 SEQ = ("x", "y", "c")
 
@@ -29,7 +33,8 @@
     heads = range(HEADS)
     inv_root = 1.0 / math.sqrt(DH)
     n = n_ref[...]
-    kv = [dot(n, w_refs[h][...], ((1,), (0,))).astype(BF) for h in heads]
+    pairs = [jnp.concatenate([w_ref[:ENC], w_ref[ENC:]], 1) for w_ref in w_refs]
+    kv = [dot(n, pairs[h], ((1,), (0,))).astype(BF) for h in heads]
     scores = [
         dot(q_ref[:, h * DH : (h + 1) * DH], kv[h][:, :DH], ((1,), (1,))) * inv_root for h in heads
     ]
@@ -81,7 +86,7 @@
     for operand in operands:
         if isinstance(operand, list):
             flat += operand
-            specs += [pl.BlockSpec(array.shape, lambda i, _: (0, 0)) for array in operand]
+            specs += [pl.BlockSpec((2 * ENC, DH), lambda i, _: (0, 0)) for array in operand]
         else:
             flat.append(operand)
             specs.append(spec(operand))
@@ -95,7 +100,7 @@
             out_specs=[spec(array) for array in out_shapes],
         ),
         out_shape=out_shapes,
-        compiler_params=pltpu.CompilerParams(vmem_limit_bytes=40 * 1024 * 1024),
+        compiler_params=PARAMS,
         cost_estimate=pl.CostEstimate(
             flops=flops,
             bytes_accessed=sum(array.size * array.dtype.itemsize for array in arrays),
@@ -104,7 +109,7 @@
     )(lax.axis_index("y").reshape(1), *flat, *others)
 
 
-def forward(q, n_rows, w_pairs, *others):
+def forward(q, n_rows, w_ins, *others):
     rows, cols = q.shape
     out_shapes = [
         jax.ShapeDtypeStruct((n_rows.shape[0], 2 * cols), BF),
@@ -113,7 +118,7 @@
     ]
     flops = 4 * rows * SPAN * cols + 4 * n_rows.size * cols
     return over_stretches(
-        forward_kernel, [q, n_rows, w_pairs], others, out_shapes, flops, rows * SPAN * HEADS
+        forward_kernel, [q, n_rows, w_ins], others, out_shapes, flops, rows * SPAN * HEADS
     )
 
 
@@ -126,6 +131,51 @@
     ]
     flops = 8 * q.shape[0] * SPAN * q.shape[1]
     return over_stretches(backward_kernel, [q, g, kv, probs], [], out_shapes, flops)
+
+
+def project_kernel(count, a_ref, *refs):
+    out_ref, total = refs[-2], refs[-1]
+    step = pl.program_id(0)
+    w = jnp.concatenate([w_ref[...] for w_ref in refs[:count]], 0)
+    term = dot(a_ref[...], w, ((1,), (1,)))
+
+    @pl.when(step == 0)
+    def _():
+        total[...] = term
+
+    @pl.when(step > 0)
+    def _():
+        total[...] += term
+
+    @pl.when(step == pl.num_programs(0) - 1)
+    def _():
+        out_ref[...] = total[...].astype(BF)
+
+
+def project(array, blocks, *others):
+    rows, depth = array.shape
+    size = depth // PARTS
+    cols = sum(block.shape[0] for block in blocks)
+    return pl.pallas_call(
+        functools.partial(project_kernel, len(blocks)),
+        grid=(PARTS,),
+        in_specs=[pl.BlockSpec((rows, size), lambda i: (0, i))]
+        + [pl.BlockSpec((block.shape[0], size), lambda i: (0, i)) for block in blocks]
+        + [ANYWHERE] * len(others),
+        out_specs=pl.BlockSpec((rows, cols), lambda i: (0, 0)),
+        out_shape=jax.ShapeDtypeStruct((rows, cols), BF),
+        scratch_shapes=[pltpu.VMEM((rows, cols), jnp.float32)],
+        compiler_params=pltpu.CompilerParams(vmem_limit_bytes=56 * 1024 * 1024),
+        cost_estimate=product_cost(rows, cols, depth),
+    )(array, *blocks, *others)
+
+
+def product_cost(rows, cols, depth):
+    return pl.CostEstimate(
+        flops=2 * rows * cols * depth,
+        bytes_accessed=2 * (rows * cols + rows * depth + cols * depth),
+        transcendentals=0,
+    )
 
 
 def hop(array, axis, step):
@@ -178,13 +228,14 @@
     return total.astype(BF)
 
 
-def sum_kernel(in_ref, *out_refs):
+def sum_kernel(in_ref, *refs):
+    out_refs = refs[-2:]
     total = jnp.sum(in_ref[...].astype(jnp.float32), 0).astype(BF)
     for i in range(2):
         out_refs[i][...] = total[:, i * DH : (i + 1) * DH]
 
 
-def sum_pair(array):
+def sum_pair(array, *others):
     n = lax.axis_size("z")
     terms = lax.all_to_all(array, "z", split_axis=0, concat_axis=0, tiled=True)
     rows, cols = array.shape[0] // n, array.shape[1]
@@ -192,13 +243,13 @@
     return pl.pallas_call(
         sum_kernel,
         grid=(4,),
-        in_specs=[pl.BlockSpec((n, size, cols), lambda i: (0, i, 0))],
+        in_specs=[pl.BlockSpec((n, size, cols), lambda i: (0, i, 0))] + [ANYWHERE] * len(others),
         out_specs=[pl.BlockSpec((size, DH), lambda i: (i, 0))] * 2,
         out_shape=[jax.ShapeDtypeStruct((rows, DH), BF)] * 2,
         cost_estimate=pl.CostEstimate(
             flops=array.size, bytes_accessed=2 * array.size, transcendentals=0
         ),
-    )(terms.reshape(n, rows, cols))
+    )(terms.reshape(n, rows, cols), *others)
 
 
 def sum_parts(array, axis):
@@ -214,13 +265,6 @@
     start = lax.rem(n - lax.axis_index("z"), n) * size
     twice = jnp.concatenate(blocks + blocks[:-1], 0)
     return lax.dynamic_slice_in_dim(twice, start, n * size, 0).astype(jnp.float32)
-
-
-def z_spread(block):
-    n = lax.axis_size("z")
-    copies = jnp.broadcast_to(block[None], (n,) + block.shape).reshape((-1,) + block.shape[1:])
-    blocks = lax.all_to_all(copies, "z", split_axis=0, concat_axis=0, tiled=True)
-    return blocks.astype(jnp.float32)
 
 
 def shift(block):
@@ -259,7 +303,7 @@
 
 
 def shards(tokens, grad_in, enc_store, nbr_owner, nbr_row, w_query, w_key, w_value, w_out):
-    w_pair = jnp.concatenate([w_key, w_value], 1)
+    w_in = jnp.concatenate([w_key, w_value, w_query], 0)
     first = lax.axis_index(SEQ) * NBRS
     owners = lax.dynamic_slice_in_dim(nbr_owner, first, NBRS, 1)
     rows = lax.dynamic_slice_in_dim(nbr_row, first, NBRS, 1)
@@ -267,39 +311,37 @@
     from_units = own * NBRS + jnp.arange(NBRS, dtype=jnp.int32)
 
     t_own = shift(tokens)
-    q_near = near(w_query, "y")
+    in_near = near(w_in, "y")
     t_rows = lax.all_gather(t_own, ROWS, axis=0, tiled=True)
     g_own = shift(grad_in)
     outgoing = pick(enc_store, rows.reshape(-1), t_own)
     arrived = lax.all_to_all(outgoing, "z", split_axis=0, concat_axis=0, tiled=True)
-    units = pick(arrived, from_units, t_rows, q_near, g_own)
+    units = pick(arrived, from_units, t_rows, in_near, g_own)
     n_rows = lax.all_gather(units, ROWS, axis=0, tiled=True).reshape(-1, ENC)
-    pair_near = near(w_pair, "y")
-    q_far = far(*q_near, "y")
-    pair_far = far(*pair_near, "y")
-    out_near = near(after(w_out, q_near), "y")
-    g_own = after(g_own, n_rows, q_far, out_near)
+    in_far = far(*in_near, "y")
+    out_near = near(after(w_out, in_near), "y")
+    g_own = after(g_own, n_rows, in_far)
     g_rows = lax.all_gather(g_own, ROWS, axis=0, tiled=True)
-    wq = jnp.concatenate([w_query, q_near[0], q_far, q_near[1]], 1)
+    w_ins = [w_in, in_near[0], in_far, in_near[1]]
+    wq = jnp.concatenate([block[2 * ENC :] for block in w_ins], 1)
     q = dot(t_rows, wq, ((1,), (0,))).astype(BF)
-    w_pairs = [w_pair, pair_near[0], pair_far, pair_near[1]]
-    kv, probs, ctx = forward(q, n_rows, w_pairs)
+    kv, probs, ctx = forward(q, n_rows, w_ins, out_near)
     half = w_out.shape[0] // 2
     out_far = [hop(out_near[0][:half], "y", -1), hop(out_near[1][half:], "y", 1)]
     d_out = dot(after(ctx, out_far), g_rows, ((0,), (0,))).astype(BF)
-    wo = jnp.concatenate([w_out, out_near[0], *out_far, out_near[1]], 0)
-    g = dot(g_rows, after(wo, d_out), ((1,), (1,))).astype(BF)
+    g = project(g_rows, [w_out, out_near[0], *out_far, out_near[1]], d_out)
     dq, early, late, dkv = backward(q, g, kv, probs)
     early = dot(t_rows, early, ((0,), (0,))).astype(BF)
     term = dot(after(dq, early), wq, ((1,), (1,))).astype(BF)
     d_pair = dot(after(dkv, term), n_rows, ((0,), (0,))).astype(BF)
-    early = sum_pair(early)
-    late = sum_pair(after(dot(t_rows, late, ((0,), (0,))).astype(BF), early, d_pair))
+    late = dot(t_rows, late, ((0,), (0,))).astype(BF)
+    early = sum_pair(early, late)
+    late = sum_pair(after(late, early, d_pair))
 
     d_out = lax.psum_scatter(d_out, "y", scatter_dimension=0, tiled=True)
     d_pair = lax.psum_scatter(after(d_pair, d_out, early), "y", scatter_dimension=0, tiled=True)
-    late = after(late, d_pair)
-    term = lax.psum_scatter(after(term, d_pair), ROWS, scatter_dimension=0, tiled=True)
+    late, term = after((late, term), d_pair)
+    term = lax.psum_scatter(term, ROWS, scatter_dimension=0, tiled=True)
     d_query = reduce_ring([late[1], early[1], early[0], late[0]], "y")
     width = d_out.shape[1]
     d_pair = d_pair.reshape(4, -1, 2, ENC)

time: 328 us -> 314 us (0.957); the launches traced: 322 us -> 313 us
  matrix products: 40.5 us -> 29.4 us
  Pallas kernels: 29.6 us -> 39.4 us
  local copies, waits for them, and re-layouts: 38 us -> 31.3 us
  starting transfers between devices: 65.3 us -> 59.3 us
  waiting for transfers between devices: 125 us -> 129 us
    dot_general x7 -> x6, matrix products: 40.5 us -> 29.4 us  [dot(): lax.dot_general(left, right, (dims, ((), ())), preferred_element_type=jnp...]
    ppermute x24 -> x20, starting transfers between devices: 36.6 us -> 29.3 us  [hop(): return lax.ppermute(array, axis, [(i, (i + step) % n) for i in range(n)])]
    pallas_call x0 -> x1, Pallas kernels: none -> 7.24 us  [project(): pl.pallas_call(functools.partial(project_kernel, len(blocks)), grid=(PART...]
    unnamed x88 -> x99, local copies, waits for them, and re-layouts: 24.4 us -> 17.9 us
    ppermute x2, waiting for transfers between devices: 21.3 us -> 15 us  [shift(): later = lax.ppermute(block, SEQ, [(i, i - 1) for i in range(1, n)])]
    all_gather x1, waiting for transfers between devices: 0.02 us -> 6 us  [shards(): n_rows = lax.all_gather(units, ROWS, axis=0, tiled=True).reshape(-1, ENC)]
    ppermute x24 -> x20, waiting for transfers between devices: 64.9 us -> 64.4 us  [hop(): return lax.ppermute(array, axis, [(i, (i + step) % n) for i in range(n)])]
  transfers between devices with their start and end apart: 37 -> 33, of which waited for: 18 -> 17; matrix products, arithmetic and copies ran while one was open for 21% -> 17% of each run, Pallas kernels for 8% -> 12%
where the time goes in v2:
time: 314 us; the launch traced here: 313 us
  waiting for transfers between devices  129 us (41%)
  starting transfers between devices  59.3 us (19%)
  Pallas kernels  39.4 us (13%)
  local copies, waits for them, and re-layouts  31.3 us (10%)
  matrix products  29.4 us (9%)
  between operations  14.9 us (5%)
  other arithmetic  9.02 us (3%)
    ppermute x20, waiting for transfers between devices, hop(): return lax.ppermute(array, axis, [(i, (i + step) % n) for i in range(n)])  64.4 us
    dot_general x6, matrix products, dot(): lax.dot_general(left, right, (dims, ((), ())), preferred_element_type=jnp...  29.4 us
    ppermute x20, starting transfers between devices, hop(): return lax.ppermute(array, axis, [(i, (i + step) % n) for i in range(n)])  29.3 us
    all_to_all x2, waiting for transfers between devices, sum_pair(): terms = lax.all_to_all(array, 'z', split_axis=0, concat_axis=0, tiled=True)  27.1 us
    unnamed x99, local copies, waits for them, and re-layouts  17.9 us
    pallas_call x2, Pallas kernels, over_stretches(): pl.pallas_call(kernel, grid_spec=pltpu.PrefetchScalarGridSpec(num_scalar_...  16.3 us
    ppermute x2, waiting for transfers between devices, shift(): later = lax.ppermute(block, SEQ, [(i, i - 1) for i in range(1, n)])  15 us
    ppermute x2, starting transfers between devices, shift(): later = lax.ppermute(block, SEQ, [(i, i - 1) for i in range(1, n)])  10.6 us
  transfers between devices with their start and end apart: 33, of which 17 were waited for; matrix products, arithmetic and copies ran while one was open for 17% of the time, Pallas kernels for 12%

profile of v2, /device:TPU:2, one launch (start us, length us, event | category | flops | bytes accessed | tf_op | source)
XLA Modules:
  0.0 312.6 jit_solution(7001963912446183299)
XLA Ops:
  7.2 4.5 %collective-permute-start = (bf16[64,4096]{1,0:T(8,128)(2,1)}, bf16[64,4096]{1,0:T(8,128)(2,1)S(1)}, u32[]{:S(2)}, u32[]{:S(2)}) collective-permute-start(bf16[64,4096]{1,0:T(8,128)(2,1)} %param.9), channel_id=1, source_target_pairs={{1,0},{2,1},{3,2},{4,3},{5,4},{6,5},{7,6},{8,7},{9,8},{10,9},{11,1... | collective-permute-start | bytes 1572872 | tf_op jit(solution)/shard_map/ppermute | solution.py:272
  12.6 6.1 %collective-permute-done = bf16[64,4096]{1,0:T(8,128)(2,1)S(1)} collective-permute-done((bf16[64,4096]{1,0:T(8,128)(2,1)}, bf16[64,4096]{1,0:T(8,128)(2,1)S(1)}, u32[]{:S(2)}, u32[]{:S(2)}) %collective-permute-start) | collective-permute-done | bytes 524320 | tf_op jit(solution)/shard_map/ppermute | solution.py:272
  26.7 6.4 %shard_map.128 = bf16[8,128,896]{2,1,0:T(8,128)(2,1)} custom-call(s32[8]{0:T(128)} %reshape.46.ids_ref, bf16[4,128,896]{2,1,0:T(8,128)(2,1)} %in_ref.1, bf16[64,4096]{1,0:T(8,128)(2,1)} %pad_maximum_fusion.5.refs_0_), custom_call_target="tpu_custom_call" | custom-call | bytes 3670016 | tf_op jit(solution)/shard_map/pallas_call | solution.py:289
  33.0 5.3 %all-to-all-start = ((bf16[8,128,896]{2,1,0:T(8,128)(2,1)}), bf16[8,128,896]{2,1,0:T(8,128)(2,1)}, u32[]{:S(2)}, u32[]{:S(2)}) async-start(bf16[8,128,896]{2,1,0:T(8,128)(2,1)} %shard_map.128), calls=%async_computation | async-start | bytes 3670016 | tf_op jit(solution)/shard_map/all_to_all | solution.py:318
  38.4 6.2 %collective-permute-start.5 = (bf16[64,4096]{1,0:T(8,128)(2,1)}, bf16[64,4096]{1,0:T(8,128)(2,1)S(1)}, u32[]{:S(2)}, u32[]{:S(2)}) collective-permute-start(bf16[64,4096]{1,0:T(8,128)(2,1)} %param.10), channel_id=1, source_target_pairs={{1,0},{2,1},{3,2},{4,3},{5,4},{6,5},{7,6},{8,7},{9,8},{10,9},{11,1... | collective-permute-start | bytes 1572872 | tf_op jit(solution)/shard_map/ppermute | solution.py:272
  47.3 8.9 %collective-permute-done.5 = bf16[64,4096]{1,0:T(8,128)(2,1)S(1)} collective-permute-done((bf16[64,4096]{1,0:T(8,128)(2,1)}, bf16[64,4096]{1,0:T(8,128)(2,1)S(1)}, u32[]{:S(2)}, u32[]{:S(2)}) %collective-permute-start.5) | collective-permute-done | bytes 524320 | tf_op jit(solution)/shard_map/ppermute | solution.py:272
  58.0 3.5 %collective-permute-done.1.refs_1_ = bf16[5888,128]{1,0:T(8,128)(2,1)S(1)} collective-permute-done((bf16[5888,128]{1,0:T(8,128)(2,1)}, bf16[5888,128]{1,0:T(8,128)(2,1)S(1)}, u32[]{:S(2)}, u32[]{:S(2)}) %collective-permute-start.1) | collective-permute-done | bytes 1507360 | tf_op jit(solution)/shard_map/ppermute | solution.py:183
  66.8 5.0 %collective-permute-start.2 = (bf16[2944,128]{1,0:T(8,128)(2,1)S(1)}, bf16[2944,128]{1,0:T(8,128)(2,1)S(1)}, u32[]{:S(2)}, u32[]{:S(2)}) collective-permute-start(bf16[2944,128]{1,0:T(8,128)(2,1)S(1)} %slice.122), channel_id=1, source_target_pairs={{0,6},{2,0},{4,2},{6,4},{1,7},{3,1},{5,3},{7,5},{8,14},{10,8},{12,... | collective-permute-start | bytes 2261000 | tf_op jit(solution)/shard_map/ppermute | solution.py:183
  73.0 15.8 %collective-permute-done.2 = bf16[2944,128]{1,0:T(8,128)(2,1)S(1)} collective-permute-done((bf16[2944,128]{1,0:T(8,128)(2,1)S(1)}, bf16[2944,128]{1,0:T(8,128)(2,1)S(1)}, u32[]{:S(2)}, u32[]{:S(2)}) %collective-permute-start.2) | collective-permute-done | bytes 753696 | tf_op jit(solution)/shard_map/ppermute | solution.py:183
  88.9 4.9 %collective-permute-done.4 = bf16[2944,128]{1,0:T(8,128)(2,1)S(1)} collective-permute-done((bf16[2944,128]{1,0:T(8,128)(2,1)S(1)}, bf16[2944,128]{1,0:T(8,128)(2,1)S(1)}, u32[]{:S(2)}, u32[]{:S(2)}) %collective-permute-start.4) | collective-permute-done | bytes 753696 | tf_op jit(solution)/shard_map/ppermute | solution.py:183
  93.9 6.0 %all-gather.6.cloned.1.call-done = bf16[16,128,896]{2,1,0:T(8,128)(2,1)} async-done(((bf16[2,128,896]{2,1,0:T(8,128)(2,1)}), bf16[16,128,896]{2,1,0:T(8,128)(2,1)}) %all-gather.6.cloned.1.call-update) | async-done | bytes 3670032 | tf_op jit(solution)/shard_map/all_gather | solution.py:320
  105.2 22.8 %collective-permute-done.6.refs_4_.refs_1_ = bf16[128,4096]{1,0:T(8,128)(2,1)S(1)} collective-permute-done((bf16[128,4096]{1,0:T(8,128)(2,1)}, bf16[128,4096]{1,0:T(8,128)(2,1)S(1)}, u32[]{:S(2)}, u32[]{:S(2)}) %collective-permute-start.6) | collective-permute-done | bytes 1048608 | tf_op jit(solution)/shard_map/ppermute | solution.py:183
  128.1 3.7 %collective-permute-start.7 = (bf16[64,4096]{1,0:T(8,128)(2,1)S(1)}, bf16[64,4096]{1,0:T(8,128)(2,1)}, u32[]{:S(2)}, u32[]{:S(2)}) collective-permute-start(bf16[64,4096]{1,0:T(8,128)(2,1)S(1)} %slice.127), channel_id=1, source_target_pairs={{0,6},{2,0},{4,2},{6,4},{1,7},{3,1},{5,3},{7,5},{8,14},{10,8},{12,... | collective-permute-start | bytes 1572872 | tf_op jit(solution)/shard_map/ppermute | solution.py:183
  134.4 11.4 %shard_map.132 = (bf16[2048,1024]{1,0:T(8,128)(2,1)}, f32[8,4,64,256]{3,2,1,0:T(8,128)S(1)}, bf16[512,512]{1,0:T(8,128)(2,1)S(1)}) custom-call(s32[1]{0:T(128)} %bitcast.place_ref, bf16[512,512]{1,0:T(8,128)(2,1)S(1)} %convolution_convert_fusion.5.q_ref, bf16[2048,896]{1,0:T(8,128)(2,1)} %bitcast.33, ...), custom_call_target="tpu_custom_call" | custom-call | flops 4026531840 | bytes 17039360 | tf_op jit(solution)/shard_map/pallas_call | solution.py:94
  148.0 6.8 %convolution_convert_fusion.1.refs_5_ = bf16[512,4096]{1,0:T(8,128)(2,1)} fusion(bf16[512,512]{1,0:T(8,128)(2,1)} %shard_map.133, bf16[512,4096]{1,0:T(8,128)(2,1)} %all-gather.8.cloned.1.call-done.a_ref), kind=kOutput, calls=%fused_computation.1 | convolution fusion | flops 2149580800 | bytes 8912896 | tf_op jit(solution)/shard_map/dot_general | solution.py:28
  154.8 7.2 %shard_map.134.g_ref = bf16[512,512]{1,0:T(8,128)(2,1)} custom-call(bf16[512,4096]{1,0:T(8,128)(2,1)} %all-gather.8.cloned.1.call-done.a_ref, bf16[128,4096]{1,0:T(8,128)(2,1)} %refs_0_.2, bf16[128,4096]{1,0:T(8,128)(2,1)} %copy-done.10, bf16[64,4096]{1,0:T(8,128)(2,1)} %collective-permute-done.7.refs_1_.refs_2_, ...), custom_call_target="tpu_custom_call" | custom-call | flops 2147483648 | bytes 8912896 | tf_op jit(solution)/shard_map/pallas_call | solution.py:159
  163.1 4.9 %shard_map.135 = (bf16[512,512]{1,0:T(8,128)(2,1)S(1)}, bf16[512,256]{1,0:T(8,128)(2,1)S(1)}, bf16[512,256]{1,0:T(8,128)(2,1)S(1)}, bf16[2048,1024]{1,0:T(8,128)(2,1)S(1)}) custom-call(s32[1]{0:T(128)} %bitcast.place_ref, bf16[512,512]{1,0:T(8,128)(2,1)S(1)} %convolution_convert_fusion.5.q_ref, bf16[512,512]{1,0:T(8,128)(2,1)S(1)} %copy-done.15, ...), custom_call_target="tpu_custom_call" | custom-call | flops 536870912 | bytes 12582912 | tf_op jit(solution)/shard_map/pallas_call | solution.py:94
  170.9 4.6 %all-to-all-start.1 = ((bf16[4,1024,256]{2,1,0:T(8,128)(2,1)}), bf16[4,1024,256]{2,1,0:T(8,128)(2,1)S(1)}, u32[]{:S(2)}, u32[]{:S(2)}) async-start(bf16[4,1024,256]{2,1,0:T(8,128)(2,1)} %bitcast.29), calls=%async_computation.1 | async-start | bytes 4194304 | tf_op jit(solution)/shard_map/all_to_all | solution.py:240
  175.4 6.7 %convolution_convert_fusion.refs_1_.refs_2_ = bf16[512,4096]{1,0:T(8,128)(2,1)} fusion(bf16[512,512]{1,0:T(8,128)(2,1)S(1)} %copy-done.17, bf16[4096,128]{1,0:T(8,128)(2,1)} %copy-done.36, bf16[4096,128]{1,0:T(8,128)(2,1)} %copy-done.37, bf16[4096,128]{1,0:T(8,128)(2,1)} %copy-done.35, bf16[4096,128]{1,0:T(8,128)(2,1)} %param.14), kind=kOutput, calls=%fused_computation | convolution fusion | flops 2166358016 | bytes 8912896 | tf_op jit(solution)/shard_map/dot_general | solution.py:28
  182.2 8.1 %convolution_convert_fusion.4.refs_3_ = bf16[1024,896]{1,0:T(8,128)(2,1)S(1)} fusion(bf16[2048,1024]{1,0:T(8,128)(2,1)} %shard_map.138, bf16[2048,896]{1,0:T(8,128)(2,1)} %bitcast.34), kind=kOutput, calls=%fused_computation.5 | convolution fusion | flops 3759013888 | bytes 9699328 | tf_op jit(solution)/shard_map/dot_general | solution.py:28
  194.7 6.4 %all-to-all-done.1.in_ref = bf16[4,1024,256]{2,1,0:T(8,128)(2,1)S(1)} async-done(((bf16[4,1024,256]{2,1,0:T(8,128)(2,1)}), bf16[4,1024,256]{2,1,0:T(8,128)(2,1)S(1)}, u32[]{:S(2)}, u32[]{:S(2)}) %all-to-all-start.1) | async-done | bytes 2097184 | tf_op jit(solution)/shard_map/all_to_all | solution.py:240
  202.4 3.5 %shard_map.136 = (bf16[1024,128]{1,0:T(8,128)(2,1)}, bf16[1024,128]{1,0:T(8,128)(2,1)}) custom-call(bf16[4,1024,256]{2,1,0:T(8,128)(2,1)} %copy-done.18, bf16[4096,256]{1,0:T(8,128)(2,1)} %convolution_convert_fusion.3.refs_0_), custom_call_target="tpu_custom_call" | custom-call | flops 1048576 | bytes 2097152 | tf_op jit(solution)/shard_map/pallas_call | solution.py:243
  206.0 3.8 %all-to-all-start.2 = ((bf16[4,1024,256]{2,1,0:T(8,128)(2,1)}), bf16[4,1024,256]{2,1,0:T(8,128)(2,1)S(1)}, u32[]{:S(2)}, u32[]{:S(2)}) async-start(bf16[4,1024,256]{2,1,0:T(8,128)(2,1)} %bitcast.28), calls=%async_computation.2 | async-start | bytes 4194304 | tf_op jit(solution)/shard_map/all_to_all | solution.py:240
  210.4 3.2 %collective-permute-start.13 = (bf16[512,128]{1,0:T(8,128)(2,1)S(1)}, bf16[512,128]{1,0:T(8,128)(2,1)S(1)}, u32[]{:S(2)}, u32[]{:S(2)}) collective-permute-start(bf16[512,128]{1,0:T(8,128)(2,1)S(1)} %get-tuple-element.52), channel_id=1, source_target_pairs={{0,6},{2,0},{4,2},{6,4},{1,7},{3,1},{5,3},{7,5},{8,14},{10,8},{12,... | collective-permute-start | bytes 393224 | tf_op jit(solution)/shard_map/ppermute | solution.py:183
  213.7 20.7 %all-to-all-done.2.in_ref = bf16[4,1024,256]{2,1,0:T(8,128)(2,1)S(1)} async-done(((bf16[4,1024,256]{2,1,0:T(8,128)(2,1)}), bf16[4,1024,256]{2,1,0:T(8,128)(2,1)S(1)}, u32[]{:S(2)}, u32[]{:S(2)}) %all-to-all-start.2) | async-done | bytes 2097184 | tf_op jit(solution)/shard_map/all_to_all | solution.py:240
  235.7 3.5 %shard_map.140 = (bf16[1024,128]{1,0:T(8,128)(2,1)}, bf16[1024,128]{1,0:T(8,128)(2,1)}) custom-call(bf16[4,1024,256]{2,1,0:T(8,128)(2,1)} %copy-done.19), custom_call_target="tpu_custom_call" | custom-call | flops 1048576 | bytes 2097152 | tf_op jit(solution)/shard_map/pallas_call | solution.py:243
  242.4 3.7 %all-to-all-start.3 = ((bf16[4,32,5888]{2,1,0:T(8,128)(2,1)}), bf16[4,32,5888]{2,1,0:T(8,128)(2,1)S(1)}, u32[]{:S(2)}, u32[]{:S(2)}) async-start(bf16[4,32,5888]{2,1,0:T(8,128)(2,1)} %shard_map.143), calls=%async_computation.6 | async-start | bytes 3014656 | tf_op jit(solution)/shard_map/all_to_all | solution.py:256
  246.4 3.3 %collective-permute-start.14 = (bf16[1024,128]{1,0:T(8,128)(2,1)S(1)}, bf16[1024,128]{1,0:T(8,128)(2,1)S(1)}, u32[]{:S(2)}, u32[]{:S(2)}) collective-permute-start(bf16[1024,128]{1,0:T(8,128)(2,1)S(1)} %pad_maximum_fusion.9), channel_id=1, source_target_pairs={{0,6},{2,0},{4,2},{6,4},{1,7},{3,1},{5,3},{7,5},{8,14},{10,8},{12,... | collective-permute-start | bytes 786440 | tf_op jit(solution)/shard_map/ppermute | solution.py:183
  249.7 4.2 %collective-permute-done.12 = bf16[1024,128]{1,0:T(8,128)(2,1)S(1)} collective-permute-done((bf16[1024,128]{1,0:T(8,128)(2,1)S(1)}, bf16[1024,128]{1,0:T(8,128)(2,1)S(1)}, u32[]{:S(2)}, u32[]{:S(2)}) %collective-permute-start.12) | collective-permute-done | bytes 262176 | tf_op jit(solution)/shard_map/ppermute | solution.py:183
  254.7 8.9 %all-to-all-done.3 = bf16[4,32,5888]{2,1,0:T(8,128)(2,1)S(1)} async-done(((bf16[4,32,5888]{2,1,0:T(8,128)(2,1)}), bf16[4,32,5888]{2,1,0:T(8,128)(2,1)S(1)}, u32[]{:S(2)}, u32[]{:S(2)}) %all-to-all-start.3) | async-done | bytes 1507360 | tf_op jit(solution)/shard_map/all_to_all | solution.py:256
  270.4 8.1 %collective-permute-done.15 = bf16[1024,128]{1,0:T(8,128)(2,1)S(1)} collective-permute-done((bf16[1024,128]{1,0:T(8,128)(2,1)}, bf16[1024,128]{1,0:T(8,128)(2,1)S(1)}, u32[]{:S(2)}, u32[]{:S(2)}) %collective-permute-start.15) | collective-permute-done | bytes 262176 | tf_op jit(solution)/shard_map/ppermute | solution.py:183
  298.2 6.5 %collective-permute-done.10 = bf16[64,4096]{1,0:T(8,128)(2,1)S(1)} collective-permute-done((bf16[64,4096]{1,0:T(8,128)(2,1)}, bf16[64,4096]{1,0:T(8,128)(2,1)S(1)}, u32[]{:S(2)}, u32[]{:S(2)}) %collective-permute-start.10) | collective-permute-done | bytes 524320 | tf_op jit(solution)/shard_map/ppermute | solution.py:278
  (206 shorter events, 73.1 us)
Async XLA Ops:
  7.2 55.5 %all-gather.4.cloned.1.call-start = ((), (), s32[]{:S(2)}) async-start(), calls=%async_computation.7 | async-start | bytes 4718592 | tf_op jit(solution)/shard_map/all_gather | solution.py:315
  7.2 11.5 %collective-permute-start = (bf16[64,4096]{1,0:T(8,128)(2,1)}, bf16[64,4096]{1,0:T(8,128)(2,1)S(1)}, u32[]{:S(2)}, u32[]{:S(2)}) collective-permute-start(bf16[64,4096]{1,0:T(8,128)(2,1)} %param.9), channel_id=1, source_target_pairs={{1,0},{2,1},{3,2},{4,3},{5,4},{6,5},{7,6},{8,7},{9,8},{10,9},{11,1... | collective-permute-start | bytes 1572872 | tf_op jit(solution)/shard_map/ppermute | solution.py:272
  24.0 37.4 %collective-permute-start.1 = (bf16[5888,128]{1,0:T(8,128)(2,1)}, bf16[5888,128]{1,0:T(8,128)(2,1)S(1)}, u32[]{:S(2)}, u32[]{:S(2)}) collective-permute-start(bf16[5888,128]{1,0:T(8,128)(2,1)} %constant_dynamic-update-slice_fusion.refs_0_), channel_id=1, source_target_pairs={{0,6},{2,0},{4,2},{6,4},{1,7},{3,1},{5,3},{7,5},{8,14},{10,8},{12,... | collective-permute-start | bytes 4521992 | tf_op jit(solution)/shard_map/ppermute | solution.py:183
  24.8 36.7 %collective-permute-start.3 = (bf16[5888,128]{1,0:T(8,128)(2,1)}, bf16[5888,128]{1,0:T(8,128)(2,1)S(1)}, u32[]{:S(2)}, u32[]{:S(2)}) collective-permute-start(bf16[5888,128]{1,0:T(8,128)(2,1)} %constant_dynamic-update-slice_fusion.refs_0_), channel_id=1, source_target_pairs={{0,2},{2,4},{4,6},{6,0},{1,3},{3,5},{5,7},{7,1},{8,10},{10,12},{12... | collective-permute-start | bytes 4521992 | tf_op jit(solution)/shard_map/ppermute | solution.py:183
  33.0 29.6 %all-to-all-start = ((bf16[8,128,896]{2,1,0:T(8,128)(2,1)}), bf16[8,128,896]{2,1,0:T(8,128)(2,1)}, u32[]{:S(2)}, u32[]{:S(2)}) async-start(bf16[8,128,896]{2,1,0:T(8,128)(2,1)} %shard_map.128), calls=%async_computation | async-start | bytes 3670016 | tf_op jit(solution)/shard_map/all_to_all | solution.py:318
  38.4 61.6 %all-gather.6.cloned.1.call-start = ((), (), s32[]{:S(2)}) async-start(), calls=%async_computation.8 | async-start | bytes 4128768 | tf_op jit(solution)/shard_map/all_gather | solution.py:320
  38.4 17.9 %collective-permute-start.5 = (bf16[64,4096]{1,0:T(8,128)(2,1)}, bf16[64,4096]{1,0:T(8,128)(2,1)S(1)}, u32[]{:S(2)}, u32[]{:S(2)}) collective-permute-start(bf16[64,4096]{1,0:T(8,128)(2,1)} %param.10), channel_id=1, source_target_pairs={{1,0},{2,1},{3,2},{4,3},{5,4},{6,5},{7,6},{8,7},{9,8},{10,9},{11,1... | collective-permute-start | bytes 1572872 | tf_op jit(solution)/shard_map/ppermute | solution.py:272
  65.6 82.4 %all-gather.8.cloned.1.call-start = ((), (), s32[]{:S(2)}) async-start(), calls=%async_computation.9 | async-start | bytes 4718592 | tf_op jit(solution)/shard_map/all_gather | solution.py:324
  66.8 22.1 %collective-permute-start.2 = (bf16[2944,128]{1,0:T(8,128)(2,1)S(1)}, bf16[2944,128]{1,0:T(8,128)(2,1)S(1)}, u32[]{:S(2)}, u32[]{:S(2)}) collective-permute-start(bf16[2944,128]{1,0:T(8,128)(2,1)S(1)} %slice.122), channel_id=1, source_target_pairs={{0,6},{2,0},{4,2},{6,4},{1,7},{3,1},{5,3},{7,5},{8,14},{10,8},{12,... | collective-permute-start | bytes 2261000 | tf_op jit(solution)/shard_map/ppermute | solution.py:183
  73.0 20.9 %collective-permute-start.4 = (bf16[2944,128]{1,0:T(8,128)(2,1)S(1)}, bf16[2944,128]{1,0:T(8,128)(2,1)S(1)}, u32[]{:S(2)}, u32[]{:S(2)}) collective-permute-start(bf16[2944,128]{1,0:T(8,128)(2,1)S(1)} %slice.123), channel_id=1, source_target_pairs={{0,2},{2,4},{4,6},{6,0},{1,3},{3,5},{5,7},{7,1},{8,10},{10,12},{12... | collective-permute-start | bytes 2261000 | tf_op jit(solution)/shard_map/ppermute | solution.py:183
  100.0 105.9 %reduce-scatter.4.cloned.1.call-start = ((), (), s32[]{:S(2)}) async-start(), calls=%async_computation.10 | async-start | bytes 5242880 | tf_op jit(solution)/shard_map/reduce_scatter | solution.py:341
  102.2 25.9 %collective-permute-start.6 = (bf16[128,4096]{1,0:T(8,128)(2,1)}, bf16[128,4096]{1,0:T(8,128)(2,1)S(1)}, u32[]{:S(2)}, u32[]{:S(2)}) collective-permute-start(bf16[128,4096]{1,0:T(8,128)(2,1)} %shard_map.131), channel_id=1, source_target_pairs={{0,6},{2,0},{4,2},{6,4},{1,7},{3,1},{5,3},{7,5},{8,14},{10,8},{12,... | collective-permute-start | bytes 3145736 | tf_op jit(solution)/shard_map/ppermute | solution.py:183
  104.9 26.8 %collective-permute-start.8 = (bf16[128,4096]{1,0:T(8,128)(2,1)}, bf16[128,4096]{1,0:T(8,128)(2,1)S(1)}, u32[]{:S(2)}, u32[]{:S(2)}) collective-permute-start(bf16[128,4096]{1,0:T(8,128)(2,1)} %shard_map.131), channel_id=1, source_target_pairs={{0,2},{2,4},{4,6},{6,0},{1,3},{3,5},{5,7},{7,1},{8,10},{10,12},{12... | collective-permute-start | bytes 3145736 | tf_op jit(solution)/shard_map/ppermute | solution.py:183
  128.1 19.9 %collective-permute-start.7 = (bf16[64,4096]{1,0:T(8,128)(2,1)S(1)}, bf16[64,4096]{1,0:T(8,128)(2,1)}, u32[]{:S(2)}, u32[]{:S(2)}) collective-permute-start(bf16[64,4096]{1,0:T(8,128)(2,1)S(1)} %slice.127), channel_id=1, source_target_pairs={{0,6},{2,0},{4,2},{6,4},{1,7},{3,1},{5,3},{7,5},{8,14},{10,8},{12,... | collective-permute-start | bytes 1572872 | tf_op jit(solution)/shard_map/ppermute | solution.py:183
  131.8 16.2 %collective-permute-start.9 = (bf16[64,4096]{1,0:T(8,128)(2,1)S(1)}, bf16[64,4096]{1,0:T(8,128)(2,1)}, u32[]{:S(2)}, u32[]{:S(2)}) collective-permute-start(bf16[64,4096]{1,0:T(8,128)(2,1)S(1)} %slice.128), channel_id=1, source_target_pairs={{0,2},{2,4},{4,6},{6,0},{1,3},{3,5},{5,7},{7,1},{8,10},{10,12},{12... | collective-permute-start | bytes 1572872 | tf_op jit(solution)/shard_map/ppermute | solution.py:183
  170.9 30.2 %all-to-all-start.1 = ((bf16[4,1024,256]{2,1,0:T(8,128)(2,1)}), bf16[4,1024,256]{2,1,0:T(8,128)(2,1)S(1)}, u32[]{:S(2)}, u32[]{:S(2)}) async-start(bf16[4,1024,256]{2,1,0:T(8,128)(2,1)} %bitcast.29), calls=%async_computation.1 | async-start | bytes 4194304 | tf_op jit(solution)/shard_map/all_to_all | solution.py:240
  175.4 63.8 %reduce-scatter.6.cloned.1.call-start = ((), (), s32[]{:S(2)}) async-start(), calls=%async_computation.11 | async-start | bytes 2293760 | tf_op jit(solution)/shard_map/reduce_scatter | solution.py:342
  206.0 28.4 %all-to-all-start.2 = ((bf16[4,1024,256]{2,1,0:T(8,128)(2,1)}), bf16[4,1024,256]{2,1,0:T(8,128)(2,1)S(1)}, u32[]{:S(2)}, u32[]{:S(2)}) async-start(bf16[4,1024,256]{2,1,0:T(8,128)(2,1)} %bitcast.28), calls=%async_computation.2 | async-start | bytes 4194304 | tf_op jit(solution)/shard_map/all_to_all | solution.py:240
  210.4 35.7 %collective-permute-start.11 = (bf16[512,128]{1,0:T(8,128)(2,1)}, bf16[512,128]{1,0:T(8,128)(2,1)S(1)}, u32[]{:S(2)}, u32[]{:S(2)}) collective-permute-start(bf16[512,128]{1,0:T(8,128)(2,1)} %get-tuple-element.51), channel_id=1, source_target_pairs={{0,2},{2,4},{4,6},{6,0},{1,3},{3,5},{5,7},{7,1},{8,10},{10,12},{12... | collective-permute-start | bytes 393224 | tf_op jit(solution)/shard_map/ppermute | solution.py:183
  210.4 35.9 %collective-permute-start.13 = (bf16[512,128]{1,0:T(8,128)(2,1)S(1)}, bf16[512,128]{1,0:T(8,128)(2,1)S(1)}, u32[]{:S(2)}, u32[]{:S(2)}) collective-permute-start(bf16[512,128]{1,0:T(8,128)(2,1)S(1)} %get-tuple-element.52), channel_id=1, source_target_pairs={{0,6},{2,0},{4,2},{6,4},{1,7},{3,1},{5,3},{7,5},{8,14},{10,8},{12,... | collective-permute-start | bytes 393224 | tf_op jit(solution)/shard_map/ppermute | solution.py:183
  242.4 21.2 %all-to-all-start.3 = ((bf16[4,32,5888]{2,1,0:T(8,128)(2,1)}), bf16[4,32,5888]{2,1,0:T(8,128)(2,1)S(1)}, u32[]{:S(2)}, u32[]{:S(2)}) async-start(bf16[4,32,5888]{2,1,0:T(8,128)(2,1)} %shard_map.143), calls=%async_computation.6 | async-start | bytes 3014656 | tf_op jit(solution)/shard_map/all_to_all | solution.py:256
  246.1 45.9 %reduce-scatter.8.cloned.1.call-start = ((), (), s32[]{:S(2)}) async-start(), calls=%async_computation.12 | async-start | bytes 4718592 | tf_op jit(solution)/shard_map/reduce_scatter | solution.py:344
  246.2 7.7 %collective-permute-start.12 = (bf16[1024,128]{1,0:T(8,128)(2,1)S(1)}, bf16[1024,128]{1,0:T(8,128)(2,1)S(1)}, u32[]{:S(2)}, u32[]{:S(2)}) collective-permute-start(bf16[1024,128]{1,0:T(8,128)(2,1)S(1)} %pad_maximum_fusion.8), channel_id=1, source_target_pairs={{0,2},{2,4},{4,6},{6,0},{1,3},{3,5},{5,7},{7,1},{8,10},{10,12},{12... | collective-permute-start | bytes 786440 | tf_op jit(solution)/shard_map/ppermute | solution.py:183
  246.4 7.5 %collective-permute-start.14 = (bf16[1024,128]{1,0:T(8,128)(2,1)S(1)}, bf16[1024,128]{1,0:T(8,128)(2,1)S(1)}, u32[]{:S(2)}, u32[]{:S(2)}) collective-permute-start(bf16[1024,128]{1,0:T(8,128)(2,1)S(1)} %pad_maximum_fusion.9), channel_id=1, source_target_pairs={{0,6},{2,0},{4,2},{6,4},{1,7},{3,1},{5,3},{7,5},{8,14},{10,8},{12,... | collective-permute-start | bytes 786440 | tf_op jit(solution)/shard_map/ppermute | solution.py:183
  264.0 16.7 %collective-permute-start.19 = (bf16[32,5888]{1,0:T(8,128)(2,1)S(1)}, bf16[32,5888]{1,0:T(8,128)(2,1)S(1)}, u32[]{:S(2)}, u32[]{:S(2)}) collective-permute-start(bf16[32,5888]{1,0:T(8,128)(2,1)S(1)} %reduce_sum.12.refs_1_), channel_id=1, source_target_pairs={{0,96},{32,0},{64,32},{96,64},{1,97},{33,1},{65,33},{97,65},{2,98}... | collective-permute-start | bytes 1130504 | tf_op jit(solution)/shard_map/ppermute | solution.py:183
  265.1 18.0 %collective-permute-start.21 = (bf16[32,5888]{1,0:T(8,128)(2,1)S(1)}, bf16[32,5888]{1,0:T(8,128)(2,1)S(1)}, u32[]{:S(2)}, u32[]{:S(2)}) collective-permute-start(bf16[32,5888]{1,0:T(8,128)(2,1)S(1)} %reduce_sum.12.refs_1_), channel_id=1, source_target_pairs={{0,32},{32,64},{64,96},{96,0},{1,33},{33,65},{65,97},{97,1},{2,34}... | collective-permute-start | bytes 1130504 | tf_op jit(solution)/shard_map/ppermute | solution.py:183
  266.1 12.4 %collective-permute-start.15 = (bf16[1024,128]{1,0:T(8,128)(2,1)}, bf16[1024,128]{1,0:T(8,128)(2,1)S(1)}, u32[]{:S(2)}, u32[]{:S(2)}) collective-permute-start(bf16[1024,128]{1,0:T(8,128)(2,1)} %shard_map.144), channel_id=1, source_target_pairs={{0,96},{32,0},{64,32},{96,64},{1,97},{33,1},{65,33},{97,65},{2,98}... | collective-permute-start | bytes 786440 | tf_op jit(solution)/shard_map/ppermute | solution.py:183
  268.4 11.3 %collective-permute-start.17 = (bf16[1024,128]{1,0:T(8,128)(2,1)}, bf16[1024,128]{1,0:T(8,128)(2,1)S(1)}, u32[]{:S(2)}, u32[]{:S(2)}) collective-permute-start(bf16[1024,128]{1,0:T(8,128)(2,1)} %shard_map.144), channel_id=1, source_target_pairs={{0,32},{32,64},{64,96},{96,0},{1,33},{33,65},{65,97},{97,1},{2,34}... | collective-permute-start | bytes 786440 | tf_op jit(solution)/shard_map/ppermute | solution.py:183
  279.7 6.2 %collective-permute-start.18 = (bf16[512,128]{1,0:T(8,128)(2,1)S(1)}, bf16[512,128]{1,0:T(8,128)(2,1)S(1)}, u32[]{:S(2)}, u32[]{:S(2)}) collective-permute-start(bf16[512,128]{1,0:T(8,128)(2,1)S(1)} %slice.134), channel_id=1, source_target_pairs={{0,32},{32,64},{64,96},{96,0},{1,33},{33,65},{65,97},{97,1},{2,34}... | collective-permute-start | bytes 393224 | tf_op jit(solution)/shard_map/ppermute | solution.py:183
  280.8 6.9 %collective-permute-start.20 = (bf16[16,5888]{1,0:T(8,128)(2,1)S(1)}, bf16[16,5888]{1,0:T(8,128)(2,1)S(1)}, u32[]{:S(2)}, u32[]{:S(2)}) collective-permute-start(bf16[16,5888]{1,0:T(8,128)(2,1)S(1)} %slice.135), channel_id=1, source_target_pairs={{0,96},{32,0},{64,32},{96,64},{1,97},{33,1},{65,33},{97,65},{2,98}... | collective-permute-start | bytes 565256 | tf_op jit(solution)/shard_map/ppermute | solution.py:183
  283.2 6.9 %collective-permute-start.22 = (bf16[16,5888]{1,0:T(8,128)(2,1)S(1)}, bf16[16,5888]{1,0:T(8,128)(2,1)S(1)}, u32[]{:S(2)}, u32[]{:S(2)}) collective-permute-start(bf16[16,5888]{1,0:T(8,128)(2,1)S(1)} %slice.136), channel_id=1, source_target_pairs={{0,32},{32,64},{64,96},{96,0},{1,33},{33,65},{65,97},{97,1},{2,34}... | collective-permute-start | bytes 565256 | tf_op jit(solution)/shard_map/ppermute | solution.py:183
  292.0 12.8 %collective-permute-start.10 = (bf16[64,4096]{1,0:T(8,128)(2,1)}, bf16[64,4096]{1,0:T(8,128)(2,1)S(1)}, u32[]{:S(2)}, u32[]{:S(2)}) collective-permute-start(bf16[64,4096]{1,0:T(8,128)(2,1)} %reduce-scatter.8.cloned.1.call-done), channel_id=1, source_target_pairs={{0,1},{1,2},{2,3},{3,4},{4,5},{5,6},{6,7},{7,8},{8,9},{9,10},{10,1... | collective-permute-start | bytes 1572872 | tf_op jit(solution)/shard_map/ppermute | solution.py:278
  (39 other events, 340.6 us)
Sparse Core Ops, SparseCore 0:
  19.8 36.7 all-gather.3
  65.7 34.2 all-gather.5
  101.7 32.0 all-gather.7
  154.9 47.9 reduce-scatter.3
  206.1 26.4 reduce-scatter.5
  249.8 34.7 reduce-scatter.7

commit v3 on v2

--- a/solution.py
+++ b/solution.py
@@ -228,28 +228,30 @@
     return total.astype(BF)
 
 
-def sum_kernel(in_ref, *refs):
-    out_refs = refs[-2:]
+def sum_kernel(in_ref, *out_refs):
     total = jnp.sum(in_ref[...].astype(jnp.float32), 0).astype(BF)
     for i in range(2):
         out_refs[i][...] = total[:, i * DH : (i + 1) * DH]
 
 
-def sum_pair(array, *others):
+def z_terms(array):
+    return lax.all_to_all(array, "z", split_axis=0, concat_axis=0, tiled=True)
+
+
+def sum_pair(terms):
     n = lax.axis_size("z")
-    terms = lax.all_to_all(array, "z", split_axis=0, concat_axis=0, tiled=True)
-    rows, cols = array.shape[0] // n, array.shape[1]
+    rows, cols = terms.shape[0] // n, terms.shape[1]
     size = rows // 4
     return pl.pallas_call(
         sum_kernel,
         grid=(4,),
-        in_specs=[pl.BlockSpec((n, size, cols), lambda i: (0, i, 0))] + [ANYWHERE] * len(others),
+        in_specs=[pl.BlockSpec((n, size, cols), lambda i: (0, i, 0))],
         out_specs=[pl.BlockSpec((size, DH), lambda i: (i, 0))] * 2,
         out_shape=[jax.ShapeDtypeStruct((rows, DH), BF)] * 2,
         cost_estimate=pl.CostEstimate(
-            flops=array.size, bytes_accessed=2 * array.size, transcendentals=0
-        ),
-    )(terms.reshape(n, rows, cols), *others)
+            flops=terms.size, bytes_accessed=2 * terms.size, transcendentals=0
+        ),
+    )(terms.reshape(n, rows, cols))
 
 
 def sum_parts(array, axis):
@@ -333,13 +335,14 @@
     dq, early, late, dkv = backward(q, g, kv, probs)
     early = dot(t_rows, early, ((0,), (0,))).astype(BF)
     term = dot(after(dq, early), wq, ((1,), (1,))).astype(BF)
-    d_pair = dot(after(dkv, term), n_rows, ((0,), (0,))).astype(BF)
     late = dot(t_rows, late, ((0,), (0,))).astype(BF)
-    early = sum_pair(early, late)
-    late = sum_pair(after(late, early, d_pair))
+    d_pair = dot(after(dkv, term, late), n_rows, ((0,), (0,))).astype(BF)
+    early_terms = z_terms(early)
+    late = sum_pair(z_terms(after(late, early_terms, d_pair)))
+    early = sum_pair(early_terms)
 
     d_out = lax.psum_scatter(d_out, "y", scatter_dimension=0, tiled=True)
-    d_pair = lax.psum_scatter(after(d_pair, d_out, early), "y", scatter_dimension=0, tiled=True)
+    d_pair = lax.psum_scatter(after(d_pair, d_out, early_terms), "y", scatter_dimension=0, tiled=True)
     late, term = after((late, term), d_pair)
     term = lax.psum_scatter(term, ROWS, scatter_dimension=0, tiled=True)
     d_query = reduce_ring([late[1], early[1], early[0], late[0]], "y")

time: 314 us -> 316 us (level)
  no operation moved by 1% of the time
where the time goes in v3:
time: 316 us; the launch traced here: 315 us
  waiting for transfers between devices  129 us (41%)
  starting transfers between devices  62.1 us (20%)
  Pallas kernels  38.9 us (12%)
  local copies, waits for them, and re-layouts  31.5 us (10%)
  matrix products  28.7 us (9%)
  between operations  14.9 us (5%)
  other arithmetic  9.02 us (3%)
    ppermute x20, waiting for transfers between devices, hop(): return lax.ppermute(array, axis, [(i, (i + step) % n) for i in range(n)])  64.7 us
    ppermute x20, starting transfers between devices, hop(): return lax.ppermute(array, axis, [(i, (i + step) % n) for i in range(n)])  30.5 us
    dot_general x6, matrix products, dot(): lax.dot_general(left, right, (dims, ((), ())), preferred_element_type=jnp...  28.7 us
    all_to_all x2, waiting for transfers between devices, z_terms(): return lax.all_to_all(array, 'z', split_axis=0, concat_axis=0, tiled=True)  25.4 us
    unnamed x99, local copies, waits for them, and re-layouts  17.2 us
    pallas_call x2, Pallas kernels, over_stretches(): pl.pallas_call(kernel, grid_spec=pltpu.PrefetchScalarGridSpec(num_scalar_...  16.3 us
    ppermute x2, waiting for transfers between devices, shift(): later = lax.ppermute(block, SEQ, [(i, i - 1) for i in range(1, n)])  15 us
    ppermute x2, starting transfers between devices, shift(): later = lax.ppermute(block, SEQ, [(i, i - 1) for i in range(1, n)])  11.1 us
  transfers between devices with their start and end apart: 33, of which 17 were waited for; matrix products, arithmetic and copies ran while one was open for 17% of the time, Pallas kernels for 12%

profile of v3, /device:TPU:2, one launch (start us, length us, event | category | flops | bytes accessed | tf_op | source)
XLA Modules:
  0.0 314.5 jit_solution(16575769791981090638)
XLA Ops:
  7.2 4.5 %collective-permute-start = (bf16[64,4096]{1,0:T(8,128)(2,1)}, bf16[64,4096]{1,0:T(8,128)(2,1)S(1)}, u32[]{:S(2)}, u32[]{:S(2)}) collective-permute-start(bf16[64,4096]{1,0:T(8,128)(2,1)} %param.9), channel_id=1, source_target_pairs={{1,0},{2,1},{3,2},{4,3},{5,4},{6,5},{7,6},{8,7},{9,8},{10,9},{11,1... | collective-permute-start | bytes 1572872 | tf_op jit(solution)/shard_map/ppermute | solution.py:274
  12.6 6.1 %collective-permute-done = bf16[64,4096]{1,0:T(8,128)(2,1)S(1)} collective-permute-done((bf16[64,4096]{1,0:T(8,128)(2,1)}, bf16[64,4096]{1,0:T(8,128)(2,1)S(1)}, u32[]{:S(2)}, u32[]{:S(2)}) %collective-permute-start) | collective-permute-done | bytes 524320 | tf_op jit(solution)/shard_map/ppermute | solution.py:274
  26.7 5.9 %shard_map.128 = bf16[8,128,896]{2,1,0:T(8,128)(2,1)} custom-call(s32[8]{0:T(128)} %reshape.46.ids_ref, bf16[4,128,896]{2,1,0:T(8,128)(2,1)} %in_ref.1, bf16[64,4096]{1,0:T(8,128)(2,1)} %pad_maximum_fusion.5.refs_0_), custom_call_target="tpu_custom_call" | custom-call | bytes 3670016 | tf_op jit(solution)/shard_map/pallas_call | solution.py:291
  32.6 5.3 %all-to-all-start = ((bf16[8,128,896]{2,1,0:T(8,128)(2,1)}), bf16[8,128,896]{2,1,0:T(8,128)(2,1)}, u32[]{:S(2)}, u32[]{:S(2)}) async-start(bf16[8,128,896]{2,1,0:T(8,128)(2,1)} %shard_map.128), calls=%async_computation | async-start | bytes 3670016 | tf_op jit(solution)/shard_map/all_to_all | solution.py:320
  37.9 6.7 %collective-permute-start.5 = (bf16[64,4096]{1,0:T(8,128)(2,1)}, bf16[64,4096]{1,0:T(8,128)(2,1)S(1)}, u32[]{:S(2)}, u32[]{:S(2)}) collective-permute-start(bf16[64,4096]{1,0:T(8,128)(2,1)} %param.10), channel_id=1, source_target_pairs={{1,0},{2,1},{3,2},{4,3},{5,4},{6,5},{7,6},{8,7},{9,8},{10,9},{11,1... | collective-permute-start | bytes 1572872 | tf_op jit(solution)/shard_map/ppermute | solution.py:274
  47.3 8.9 %collective-permute-done.5 = bf16[64,4096]{1,0:T(8,128)(2,1)S(1)} collective-permute-done((bf16[64,4096]{1,0:T(8,128)(2,1)}, bf16[64,4096]{1,0:T(8,128)(2,1)S(1)}, u32[]{:S(2)}, u32[]{:S(2)}) %collective-permute-start.5) | collective-permute-done | bytes 524320 | tf_op jit(solution)/shard_map/ppermute | solution.py:274
  58.0 3.5 %collective-permute-done.1.refs_1_ = bf16[5888,128]{1,0:T(8,128)(2,1)S(1)} collective-permute-done((bf16[5888,128]{1,0:T(8,128)(2,1)}, bf16[5888,128]{1,0:T(8,128)(2,1)S(1)}, u32[]{:S(2)}, u32[]{:S(2)}) %collective-permute-start.1) | collective-permute-done | bytes 1507360 | tf_op jit(solution)/shard_map/ppermute | solution.py:183
  66.8 5.0 %collective-permute-start.2 = (bf16[2944,128]{1,0:T(8,128)(2,1)S(1)}, bf16[2944,128]{1,0:T(8,128)(2,1)S(1)}, u32[]{:S(2)}, u32[]{:S(2)}) collective-permute-start(bf16[2944,128]{1,0:T(8,128)(2,1)S(1)} %slice.122), channel_id=1, source_target_pairs={{0,6},{2,0},{4,2},{6,4},{1,7},{3,1},{5,3},{7,5},{8,14},{10,8},{12,... | collective-permute-start | bytes 2261000 | tf_op jit(solution)/shard_map/ppermute | solution.py:183
  73.0 15.8 %collective-permute-done.2 = bf16[2944,128]{1,0:T(8,128)(2,1)S(1)} collective-permute-done((bf16[2944,128]{1,0:T(8,128)(2,1)S(1)}, bf16[2944,128]{1,0:T(8,128)(2,1)S(1)}, u32[]{:S(2)}, u32[]{:S(2)}) %collective-permute-start.2) | collective-permute-done | bytes 753696 | tf_op jit(solution)/shard_map/ppermute | solution.py:183
  88.9 4.9 %collective-permute-done.4 = bf16[2944,128]{1,0:T(8,128)(2,1)S(1)} collective-permute-done((bf16[2944,128]{1,0:T(8,128)(2,1)S(1)}, bf16[2944,128]{1,0:T(8,128)(2,1)S(1)}, u32[]{:S(2)}, u32[]{:S(2)}) %collective-permute-start.4) | collective-permute-done | bytes 753696 | tf_op jit(solution)/shard_map/ppermute | solution.py:183
  93.9 6.0 %all-gather.6.cloned.1.call-done = bf16[16,128,896]{2,1,0:T(8,128)(2,1)} async-done(((bf16[2,128,896]{2,1,0:T(8,128)(2,1)}), bf16[16,128,896]{2,1,0:T(8,128)(2,1)}) %all-gather.6.cloned.1.call-update) | async-done | bytes 3670032 | tf_op jit(solution)/shard_map/all_gather | solution.py:322
  105.2 22.8 %collective-permute-done.6.refs_4_.refs_1_ = bf16[128,4096]{1,0:T(8,128)(2,1)S(1)} collective-permute-done((bf16[128,4096]{1,0:T(8,128)(2,1)}, bf16[128,4096]{1,0:T(8,128)(2,1)S(1)}, u32[]{:S(2)}, u32[]{:S(2)}) %collective-permute-start.6) | collective-permute-done | bytes 1048608 | tf_op jit(solution)/shard_map/ppermute | solution.py:183
  128.1 3.7 %collective-permute-start.7 = (bf16[64,4096]{1,0:T(8,128)(2,1)S(1)}, bf16[64,4096]{1,0:T(8,128)(2,1)}, u32[]{:S(2)}, u32[]{:S(2)}) collective-permute-start(bf16[64,4096]{1,0:T(8,128)(2,1)S(1)} %slice.127), channel_id=1, source_target_pairs={{0,6},{2,0},{4,2},{6,4},{1,7},{3,1},{5,3},{7,5},{8,14},{10,8},{12,... | collective-permute-start | bytes 1572872 | tf_op jit(solution)/shard_map/ppermute | solution.py:183
  134.4 11.4 %shard_map.132 = (bf16[2048,1024]{1,0:T(8,128)(2,1)}, f32[8,4,64,256]{3,2,1,0:T(8,128)S(1)}, bf16[512,512]{1,0:T(8,128)(2,1)S(1)}) custom-call(s32[1]{0:T(128)} %bitcast.place_ref, bf16[512,512]{1,0:T(8,128)(2,1)S(1)} %convolution_convert_fusion.5.q_ref, bf16[2048,896]{1,0:T(8,128)(2,1)} %bitcast.33, ...), custom_call_target="tpu_custom_call" | custom-call | flops 4026531840 | bytes 17039360 | tf_op jit(solution)/shard_map/pallas_call | solution.py:94
  148.0 6.8 %convolution_convert_fusion.1.refs_5_ = bf16[512,4096]{1,0:T(8,128)(2,1)} fusion(bf16[512,512]{1,0:T(8,128)(2,1)} %shard_map.133, bf16[512,4096]{1,0:T(8,128)(2,1)} %all-gather.8.cloned.1.call-done.a_ref), kind=kOutput, calls=%fused_computation.1 | convolution fusion | flops 2149580800 | bytes 8912896 | tf_op jit(solution)/shard_map/dot_general | solution.py:28
  154.8 7.2 %shard_map.134.g_ref = bf16[512,512]{1,0:T(8,128)(2,1)} custom-call(bf16[512,4096]{1,0:T(8,128)(2,1)} %all-gather.8.cloned.1.call-done.a_ref, bf16[128,4096]{1,0:T(8,128)(2,1)} %refs_0_.2, bf16[128,4096]{1,0:T(8,128)(2,1)} %copy-done.10, bf16[64,4096]{1,0:T(8,128)(2,1)} %collective-permute-done.7.refs_1_.refs_2_, ...), custom_call_target="tpu_custom_call" | custom-call | flops 2147483648 | bytes 8912896 | tf_op jit(solution)/shard_map/pallas_call | solution.py:159
  163.1 4.9 %shard_map.135 = (bf16[512,512]{1,0:T(8,128)(2,1)S(1)}, bf16[512,256]{1,0:T(8,128)(2,1)S(1)}, bf16[512,256]{1,0:T(8,128)(2,1)S(1)}, bf16[2048,1024]{1,0:T(8,128)(2,1)S(1)}) custom-call(s32[1]{0:T(128)} %bitcast.place_ref, bf16[512,512]{1,0:T(8,128)(2,1)S(1)} %convolution_convert_fusion.5.q_ref, bf16[512,512]{1,0:T(8,128)(2,1)S(1)} %copy-done.15, ...), custom_call_target="tpu_custom_call" | custom-call | flops 536870912 | bytes 12582912 | tf_op jit(solution)/shard_map/pallas_call | solution.py:94
  170.9 4.7 %all-to-all-start.1 = ((bf16[4,1024,256]{2,1,0:T(8,128)(2,1)}), bf16[4,1024,256]{2,1,0:T(8,128)(2,1)}, u32[]{:S(2)}, u32[]{:S(2)}) async-start(bf16[4,1024,256]{2,1,0:T(8,128)(2,1)} %bitcast.3), calls=%async_computation.1 | async-start | bytes 4194304 | tf_op jit(solution)/shard_map/all_to_all | solution.py:238
  175.9 6.2 %convolution_convert_fusion.refs_1_.refs_2_ = bf16[512,4096]{1,0:T(8,128)(2,1)} fusion(bf16[512,512]{1,0:T(8,128)(2,1)S(1)} %copy-done.17, bf16[4096,128]{1,0:T(8,128)(2,1)} %copy-done.35, bf16[4096,128]{1,0:T(8,128)(2,1)} %copy-done.36, bf16[4096,128]{1,0:T(8,128)(2,1)S(1)} %copy-done.34, bf16[4096,128]{1,0:T(8,128)(2,1)S(1)} %copy-done.32), kind=kOutput, calls=%fused_computation | convolution fusion | flops 2166358016 | bytes 8912896 | tf_op jit(solution)/shard_map/dot_general | solution.py:28
  184.8 8.0 %convolution_convert_fusion.4.refs_2_ = bf16[1024,896]{1,0:T(8,128)(2,1)S(1)} fusion(bf16[2048,1024]{1,0:T(8,128)(2,1)} %shard_map.137, bf16[2048,896]{1,0:T(8,128)(2,1)} %bitcast.34), kind=kOutput, calls=%fused_computation.5 | convolution fusion | flops 3759013888 | bytes 9699328 | tf_op jit(solution)/shard_map/dot_general | solution.py:28
  194.1 7.4 %all-to-all-done.1.in_ref = bf16[4,1024,256]{2,1,0:T(8,128)(2,1)} async-done(((bf16[4,1024,256]{2,1,0:T(8,128)(2,1)}), bf16[4,1024,256]{2,1,0:T(8,128)(2,1)}, u32[]{:S(2)}, u32[]{:S(2)}) %all-to-all-start.1) | async-done | bytes 2097184 | tf_op jit(solution)/shard_map/all_to_all | solution.py:238
  202.9 4.4 %all-to-all-start.2 = ((bf16[4,1024,256]{2,1,0:T(8,128)(2,1)}), bf16[4,1024,256]{2,1,0:T(8,128)(2,1)S(1)}, u32[]{:S(2)}, u32[]{:S(2)}) async-start(bf16[4,1024,256]{2,1,0:T(8,128)(2,1)} %bitcast.29), calls=%async_computation.2 | async-start | bytes 4194304 | tf_op jit(solution)/shard_map/all_to_all | solution.py:238
  207.4 3.5 %shard_map.142 = (bf16[1024,128]{1,0:T(8,128)(2,1)}, bf16[1024,128]{1,0:T(8,128)(2,1)}) custom-call(bf16[4,1024,256]{2,1,0:T(8,128)(2,1)} %all-to-all-done.1.in_ref), custom_call_target="tpu_custom_call" | custom-call | flops 1048576 | bytes 2097152 | tf_op jit(solution)/shard_map/pallas_call | solution.py:245
  215.8 18.0 %all-to-all-done.2.in_ref = bf16[4,1024,256]{2,1,0:T(8,128)(2,1)S(1)} async-done(((bf16[4,1024,256]{2,1,0:T(8,128)(2,1)}), bf16[4,1024,256]{2,1,0:T(8,128)(2,1)S(1)}, u32[]{:S(2)}, u32[]{:S(2)}) %all-to-all-start.2) | async-done | bytes 2097184 | tf_op jit(solution)/shard_map/all_to_all | solution.py:238
  235.1 3.5 %shard_map.139 = (bf16[1024,128]{1,0:T(8,128)(2,1)}, bf16[1024,128]{1,0:T(8,128)(2,1)}) custom-call(bf16[4,1024,256]{2,1,0:T(8,128)(2,1)} %copy-done.18), custom_call_target="tpu_custom_call" | custom-call | flops 1048576 | bytes 2097152 | tf_op jit(solution)/shard_map/pallas_call | solution.py:245
  241.8 3.7 %all-to-all-start.3 = ((bf16[4,32,5888]{2,1,0:T(8,128)(2,1)}), bf16[4,32,5888]{2,1,0:T(8,128)(2,1)S(1)}, u32[]{:S(2)}, u32[]{:S(2)}) async-start(bf16[4,32,5888]{2,1,0:T(8,128)(2,1)} %shard_map.143), calls=%async_computation.6 | async-start | bytes 3014656 | tf_op jit(solution)/shard_map/all_to_all | solution.py:258
  249.1 4.8 %collective-permute-done.12 = bf16[1024,128]{1,0:T(8,128)(2,1)S(1)} collective-permute-done((bf16[1024,128]{1,0:T(8,128)(2,1)S(1)}, bf16[1024,128]{1,0:T(8,128)(2,1)S(1)}, u32[]{:S(2)}, u32[]{:S(2)}) %collective-permute-start.12) | collective-permute-done | bytes 262176 | tf_op jit(solution)/shard_map/ppermute | solution.py:183
  254.6 10.0 %all-to-all-done.3 = bf16[4,32,5888]{2,1,0:T(8,128)(2,1)S(1)} async-done(((bf16[4,32,5888]{2,1,0:T(8,128)(2,1)}), bf16[4,32,5888]{2,1,0:T(8,128)(2,1)S(1)}, u32[]{:S(2)}, u32[]{:S(2)}) %all-to-all-start.3) | async-done | bytes 1507360 | tf_op jit(solution)/shard_map/all_to_all | solution.py:258
  271.5 7.9 %collective-permute-done.15 = bf16[1024,128]{1,0:T(8,128)(2,1)S(1)} collective-permute-done((bf16[1024,128]{1,0:T(8,128)(2,1)}, bf16[1024,128]{1,0:T(8,128)(2,1)S(1)}, u32[]{:S(2)}, u32[]{:S(2)}) %collective-permute-start.15) | collective-permute-done | bytes 262176 | tf_op jit(solution)/shard_map/ppermute | solution.py:183
  281.8 3.3 %collective-permute-start.20 = (bf16[16,5888]{1,0:T(8,128)(2,1)S(1)}, bf16[16,5888]{1,0:T(8,128)(2,1)S(1)}, u32[]{:S(2)}, u32[]{:S(2)}) collective-permute-start(bf16[16,5888]{1,0:T(8,128)(2,1)S(1)} %slice.135), channel_id=1, source_target_pairs={{0,96},{32,0},{64,32},{96,64},{1,97},{33,1},{65,33},{97,65},{2,98}... | collective-permute-start | bytes 565256 | tf_op jit(solution)/shard_map/ppermute | solution.py:183
  285.2 3.2 %collective-permute-done.18 = bf16[512,128]{1,0:T(8,128)(2,1)S(1)} collective-permute-done((bf16[512,128]{1,0:T(8,128)(2,1)S(1)}, bf16[512,128]{1,0:T(8,128)(2,1)S(1)}, u32[]{:S(2)}, u32[]{:S(2)}) %collective-permute-start.18) | collective-permute-done | bytes 131104 | tf_op jit(solution)/shard_map/ppermute | solution.py:183
  300.2 6.5 %collective-permute-done.10 = bf16[64,4096]{1,0:T(8,128)(2,1)S(1)} collective-permute-done((bf16[64,4096]{1,0:T(8,128)(2,1)}, bf16[64,4096]{1,0:T(8,128)(2,1)S(1)}, u32[]{:S(2)}, u32[]{:S(2)}) %collective-permute-start.10) | collective-permute-done | bytes 524320 | tf_op jit(solution)/shard_map/ppermute | solution.py:280
  (206 shorter events, 75.2 us)
Async XLA Ops:
  7.2 54.4 %all-gather.4.cloned.1.call-start = ((), (), s32[]{:S(2)}) async-start(), calls=%async_computation.7 | async-start | bytes 4718592 | tf_op jit(solution)/shard_map/all_gather | solution.py:317
  7.2 11.5 %collective-permute-start = (bf16[64,4096]{1,0:T(8,128)(2,1)}, bf16[64,4096]{1,0:T(8,128)(2,1)S(1)}, u32[]{:S(2)}, u32[]{:S(2)}) collective-permute-start(bf16[64,4096]{1,0:T(8,128)(2,1)} %param.9), channel_id=1, source_target_pairs={{1,0},{2,1},{3,2},{4,3},{5,4},{6,5},{7,6},{8,7},{9,8},{10,9},{11,1... | collective-permute-start | bytes 1572872 | tf_op jit(solution)/shard_map/ppermute | solution.py:274
  24.0 37.4 %collective-permute-start.1 = (bf16[5888,128]{1,0:T(8,128)(2,1)}, bf16[5888,128]{1,0:T(8,128)(2,1)S(1)}, u32[]{:S(2)}, u32[]{:S(2)}) collective-permute-start(bf16[5888,128]{1,0:T(8,128)(2,1)} %constant_dynamic-update-slice_fusion.refs_0_), channel_id=1, source_target_pairs={{0,6},{2,0},{4,2},{6,4},{1,7},{3,1},{5,3},{7,5},{8,14},{10,8},{12,... | collective-permute-start | bytes 4521992 | tf_op jit(solution)/shard_map/ppermute | solution.py:183
  24.8 36.7 %collective-permute-start.3 = (bf16[5888,128]{1,0:T(8,128)(2,1)}, bf16[5888,128]{1,0:T(8,128)(2,1)S(1)}, u32[]{:S(2)}, u32[]{:S(2)}) collective-permute-start(bf16[5888,128]{1,0:T(8,128)(2,1)} %constant_dynamic-update-slice_fusion.refs_0_), channel_id=1, source_target_pairs={{0,2},{2,4},{4,6},{6,0},{1,3},{3,5},{5,7},{7,1},{8,10},{10,12},{12... | collective-permute-start | bytes 4521992 | tf_op jit(solution)/shard_map/ppermute | solution.py:183
  32.6 29.0 %all-to-all-start = ((bf16[8,128,896]{2,1,0:T(8,128)(2,1)}), bf16[8,128,896]{2,1,0:T(8,128)(2,1)}, u32[]{:S(2)}, u32[]{:S(2)}) async-start(bf16[8,128,896]{2,1,0:T(8,128)(2,1)} %shard_map.128), calls=%async_computation | async-start | bytes 3670016 | tf_op jit(solution)/shard_map/all_to_all | solution.py:320
  37.9 62.1 %all-gather.6.cloned.1.call-start = ((), (), s32[]{:S(2)}) async-start(), calls=%async_computation.8 | async-start | bytes 4128768 | tf_op jit(solution)/shard_map/all_gather | solution.py:322
  37.9 18.4 %collective-permute-start.5 = (bf16[64,4096]{1,0:T(8,128)(2,1)}, bf16[64,4096]{1,0:T(8,128)(2,1)S(1)}, u32[]{:S(2)}, u32[]{:S(2)}) collective-permute-start(bf16[64,4096]{1,0:T(8,128)(2,1)} %param.10), channel_id=1, source_target_pairs={{1,0},{2,1},{3,2},{4,3},{5,4},{6,5},{7,6},{8,7},{9,8},{10,9},{11,1... | collective-permute-start | bytes 1572872 | tf_op jit(solution)/shard_map/ppermute | solution.py:274
  65.6 82.4 %all-gather.8.cloned.1.call-start = ((), (), s32[]{:S(2)}) async-start(), calls=%async_computation.9 | async-start | bytes 4718592 | tf_op jit(solution)/shard_map/all_gather | solution.py:326
  66.8 22.1 %collective-permute-start.2 = (bf16[2944,128]{1,0:T(8,128)(2,1)S(1)}, bf16[2944,128]{1,0:T(8,128)(2,1)S(1)}, u32[]{:S(2)}, u32[]{:S(2)}) collective-permute-start(bf16[2944,128]{1,0:T(8,128)(2,1)S(1)} %slice.122), channel_id=1, source_target_pairs={{0,6},{2,0},{4,2},{6,4},{1,7},{3,1},{5,3},{7,5},{8,14},{10,8},{12,... | collective-permute-start | bytes 2261000 | tf_op jit(solution)/shard_map/ppermute | solution.py:183
  73.0 20.9 %collective-permute-start.4 = (bf16[2944,128]{1,0:T(8,128)(2,1)S(1)}, bf16[2944,128]{1,0:T(8,128)(2,1)S(1)}, u32[]{:S(2)}, u32[]{:S(2)}) collective-permute-start(bf16[2944,128]{1,0:T(8,128)(2,1)S(1)} %slice.123), channel_id=1, source_target_pairs={{0,2},{2,4},{4,6},{6,0},{1,3},{3,5},{5,7},{7,1},{8,10},{10,12},{12... | collective-permute-start | bytes 2261000 | tf_op jit(solution)/shard_map/ppermute | solution.py:183
  100.0 102.9 %reduce-scatter.4.cloned.1.call-start = ((), (), s32[]{:S(2)}) async-start(), calls=%async_computation.10 | async-start | bytes 5242880 | tf_op jit(solution)/shard_map/reduce_scatter | solution.py:344
  102.2 25.9 %collective-permute-start.6 = (bf16[128,4096]{1,0:T(8,128)(2,1)}, bf16[128,4096]{1,0:T(8,128)(2,1)S(1)}, u32[]{:S(2)}, u32[]{:S(2)}) collective-permute-start(bf16[128,4096]{1,0:T(8,128)(2,1)} %shard_map.131), channel_id=1, source_target_pairs={{0,6},{2,0},{4,2},{6,4},{1,7},{3,1},{5,3},{7,5},{8,14},{10,8},{12,... | collective-permute-start | bytes 3145736 | tf_op jit(solution)/shard_map/ppermute | solution.py:183
  104.9 26.8 %collective-permute-start.8 = (bf16[128,4096]{1,0:T(8,128)(2,1)}, bf16[128,4096]{1,0:T(8,128)(2,1)S(1)}, u32[]{:S(2)}, u32[]{:S(2)}) collective-permute-start(bf16[128,4096]{1,0:T(8,128)(2,1)} %shard_map.131), channel_id=1, source_target_pairs={{0,2},{2,4},{4,6},{6,0},{1,3},{3,5},{5,7},{7,1},{8,10},{10,12},{12... | collective-permute-start | bytes 3145736 | tf_op jit(solution)/shard_map/ppermute | solution.py:183
  128.1 19.9 %collective-permute-start.7 = (bf16[64,4096]{1,0:T(8,128)(2,1)S(1)}, bf16[64,4096]{1,0:T(8,128)(2,1)}, u32[]{:S(2)}, u32[]{:S(2)}) collective-permute-start(bf16[64,4096]{1,0:T(8,128)(2,1)S(1)} %slice.127), channel_id=1, source_target_pairs={{0,6},{2,0},{4,2},{6,4},{1,7},{3,1},{5,3},{7,5},{8,14},{10,8},{12,... | collective-permute-start | bytes 1572872 | tf_op jit(solution)/shard_map/ppermute | solution.py:183
  131.8 16.2 %collective-permute-start.9 = (bf16[64,4096]{1,0:T(8,128)(2,1)S(1)}, bf16[64,4096]{1,0:T(8,128)(2,1)}, u32[]{:S(2)}, u32[]{:S(2)}) collective-permute-start(bf16[64,4096]{1,0:T(8,128)(2,1)S(1)} %slice.128), channel_id=1, source_target_pairs={{0,2},{2,4},{4,6},{6,0},{1,3},{3,5},{5,7},{7,1},{8,10},{10,12},{12... | collective-permute-start | bytes 1572872 | tf_op jit(solution)/shard_map/ppermute | solution.py:183
  170.9 30.6 %all-to-all-start.1 = ((bf16[4,1024,256]{2,1,0:T(8,128)(2,1)}), bf16[4,1024,256]{2,1,0:T(8,128)(2,1)}, u32[]{:S(2)}, u32[]{:S(2)}) async-start(bf16[4,1024,256]{2,1,0:T(8,128)(2,1)} %bitcast.3), calls=%async_computation.1 | async-start | bytes 4194304 | tf_op jit(solution)/shard_map/all_to_all | solution.py:238
  175.6 63.0 %reduce-scatter.6.cloned.1.call-start = ((), (), s32[]{:S(2)}) async-start(), calls=%async_computation.11 | async-start | bytes 2293760 | tf_op jit(solution)/shard_map/reduce_scatter | solution.py:345
  202.9 30.8 %all-to-all-start.2 = ((bf16[4,1024,256]{2,1,0:T(8,128)(2,1)}), bf16[4,1024,256]{2,1,0:T(8,128)(2,1)S(1)}, u32[]{:S(2)}, u32[]{:S(2)}) async-start(bf16[4,1024,256]{2,1,0:T(8,128)(2,1)} %bitcast.29), calls=%async_computation.2 | async-start | bytes 4194304 | tf_op jit(solution)/shard_map/all_to_all | solution.py:238
  212.5 33.0 %collective-permute-start.11 = (bf16[512,128]{1,0:T(8,128)(2,1)}, bf16[512,128]{1,0:T(8,128)(2,1)S(1)}, u32[]{:S(2)}, u32[]{:S(2)}) collective-permute-start(bf16[512,128]{1,0:T(8,128)(2,1)} %get-tuple-element.51), channel_id=1, source_target_pairs={{0,2},{2,4},{4,6},{6,0},{1,3},{3,5},{5,7},{7,1},{8,10},{10,12},{12... | collective-permute-start | bytes 393224 | tf_op jit(solution)/shard_map/ppermute | solution.py:183
  212.8 33.1 %collective-permute-start.13 = (bf16[512,128]{1,0:T(8,128)(2,1)S(1)}, bf16[512,128]{1,0:T(8,128)(2,1)S(1)}, u32[]{:S(2)}, u32[]{:S(2)}) collective-permute-start(bf16[512,128]{1,0:T(8,128)(2,1)S(1)} %get-tuple-element.52), channel_id=1, source_target_pairs={{0,6},{2,0},{4,2},{6,4},{1,7},{3,1},{5,3},{7,5},{8,14},{10,8},{12,... | collective-permute-start | bytes 393224 | tf_op jit(solution)/shard_map/ppermute | solution.py:183
  241.8 22.8 %all-to-all-start.3 = ((bf16[4,32,5888]{2,1,0:T(8,128)(2,1)}), bf16[4,32,5888]{2,1,0:T(8,128)(2,1)S(1)}, u32[]{:S(2)}, u32[]{:S(2)}) async-start(bf16[4,32,5888]{2,1,0:T(8,128)(2,1)} %shard_map.143), calls=%async_computation.6 | async-start | bytes 3014656 | tf_op jit(solution)/shard_map/all_to_all | solution.py:258
  245.5 48.4 %reduce-scatter.8.cloned.1.call-start = ((), (), s32[]{:S(2)}) async-start(), calls=%async_computation.12 | async-start | bytes 4718592 | tf_op jit(solution)/shard_map/reduce_scatter | solution.py:347
  245.6 8.2 %collective-permute-start.12 = (bf16[1024,128]{1,0:T(8,128)(2,1)S(1)}, bf16[1024,128]{1,0:T(8,128)(2,1)S(1)}, u32[]{:S(2)}, u32[]{:S(2)}) collective-permute-start(bf16[1024,128]{1,0:T(8,128)(2,1)S(1)} %pad_maximum_fusion.8), channel_id=1, source_target_pairs={{0,2},{2,4},{4,6},{6,0},{1,3},{3,5},{5,7},{7,1},{8,10},{10,12},{12... | collective-permute-start | bytes 786440 | tf_op jit(solution)/shard_map/ppermute | solution.py:183
  246.0 7.9 %collective-permute-start.14 = (bf16[1024,128]{1,0:T(8,128)(2,1)S(1)}, bf16[1024,128]{1,0:T(8,128)(2,1)S(1)}, u32[]{:S(2)}, u32[]{:S(2)}) collective-permute-start(bf16[1024,128]{1,0:T(8,128)(2,1)S(1)} %pad_maximum_fusion.9), channel_id=1, source_target_pairs={{0,6},{2,0},{4,2},{6,4},{1,7},{3,1},{5,3},{7,5},{8,14},{10,8},{12,... | collective-permute-start | bytes 786440 | tf_op jit(solution)/shard_map/ppermute | solution.py:183
  265.0 16.8 %collective-permute-start.19 = (bf16[32,5888]{1,0:T(8,128)(2,1)S(1)}, bf16[32,5888]{1,0:T(8,128)(2,1)S(1)}, u32[]{:S(2)}, u32[]{:S(2)}) collective-permute-start(bf16[32,5888]{1,0:T(8,128)(2,1)S(1)} %reduce_sum.12.refs_1_), channel_id=1, source_target_pairs={{0,96},{32,0},{64,32},{96,64},{1,97},{33,1},{65,33},{97,65},{2,98}... | collective-permute-start | bytes 1130504 | tf_op jit(solution)/shard_map/ppermute | solution.py:183
  266.2 18.8 %collective-permute-start.21 = (bf16[32,5888]{1,0:T(8,128)(2,1)S(1)}, bf16[32,5888]{1,0:T(8,128)(2,1)S(1)}, u32[]{:S(2)}, u32[]{:S(2)}) collective-permute-start(bf16[32,5888]{1,0:T(8,128)(2,1)S(1)} %reduce_sum.12.refs_1_), channel_id=1, source_target_pairs={{0,32},{32,64},{64,96},{96,0},{1,33},{33,65},{65,97},{97,1},{2,34}... | collective-permute-start | bytes 1130504 | tf_op jit(solution)/shard_map/ppermute | solution.py:183
  267.1 12.3 %collective-permute-start.15 = (bf16[1024,128]{1,0:T(8,128)(2,1)}, bf16[1024,128]{1,0:T(8,128)(2,1)S(1)}, u32[]{:S(2)}, u32[]{:S(2)}) collective-permute-start(bf16[1024,128]{1,0:T(8,128)(2,1)} %shard_map.144), channel_id=1, source_target_pairs={{0,96},{32,0},{64,32},{96,64},{1,97},{33,1},{65,33},{97,65},{2,98}... | collective-permute-start | bytes 786440 | tf_op jit(solution)/shard_map/ppermute | solution.py:183
  269.5 12.1 %collective-permute-start.17 = (bf16[1024,128]{1,0:T(8,128)(2,1)}, bf16[1024,128]{1,0:T(8,128)(2,1)S(1)}, u32[]{:S(2)}, u32[]{:S(2)}) collective-permute-start(bf16[1024,128]{1,0:T(8,128)(2,1)} %shard_map.144), channel_id=1, source_target_pairs={{0,32},{32,64},{64,96},{96,0},{1,33},{33,65},{65,97},{97,1},{2,34}... | collective-permute-start | bytes 786440 | tf_op jit(solution)/shard_map/ppermute | solution.py:183
  281.6 6.8 %collective-permute-start.18 = (bf16[512,128]{1,0:T(8,128)(2,1)S(1)}, bf16[512,128]{1,0:T(8,128)(2,1)S(1)}, u32[]{:S(2)}, u32[]{:S(2)}) collective-permute-start(bf16[512,128]{1,0:T(8,128)(2,1)S(1)} %slice.134), channel_id=1, source_target_pairs={{0,32},{32,64},{64,96},{96,0},{1,33},{33,65},{65,97},{97,1},{2,34}... | collective-permute-start | bytes 393224 | tf_op jit(solution)/shard_map/ppermute | solution.py:183
  281.8 8.3 %collective-permute-start.20 = (bf16[16,5888]{1,0:T(8,128)(2,1)S(1)}, bf16[16,5888]{1,0:T(8,128)(2,1)S(1)}, u32[]{:S(2)}, u32[]{:S(2)}) collective-permute-start(bf16[16,5888]{1,0:T(8,128)(2,1)S(1)} %slice.135), channel_id=1, source_target_pairs={{0,96},{32,0},{64,32},{96,64},{1,97},{33,1},{65,33},{97,65},{2,98}... | collective-permute-start | bytes 565256 | tf_op jit(solution)/shard_map/ppermute | solution.py:183
  285.1 6.9 %collective-permute-start.22 = (bf16[16,5888]{1,0:T(8,128)(2,1)S(1)}, bf16[16,5888]{1,0:T(8,128)(2,1)S(1)}, u32[]{:S(2)}, u32[]{:S(2)}) collective-permute-start(bf16[16,5888]{1,0:T(8,128)(2,1)S(1)} %slice.136), channel_id=1, source_target_pairs={{0,32},{32,64},{64,96},{96,0},{1,33},{33,65},{65,97},{97,1},{2,34}... | collective-permute-start | bytes 565256 | tf_op jit(solution)/shard_map/ppermute | solution.py:183
  293.9 12.8 %collective-permute-start.10 = (bf16[64,4096]{1,0:T(8,128)(2,1)}, bf16[64,4096]{1,0:T(8,128)(2,1)S(1)}, u32[]{:S(2)}, u32[]{:S(2)}) collective-permute-start(bf16[64,4096]{1,0:T(8,128)(2,1)} %reduce-scatter.8.cloned.1.call-done), channel_id=1, source_target_pairs={{0,1},{1,2},{2,3},{3,4},{4,5},{5,6},{6,7},{7,8},{8,9},{9,10},{10,1... | collective-permute-start | bytes 1572872 | tf_op jit(solution)/shard_map/ppermute | solution.py:280
  (39 other events, 350.0 us)
Sparse Core Ops, SparseCore 0:
  19.8 37.1 all-gather.3
  65.7 34.2 all-gather.5
  101.7 32.0 all-gather.7
  154.9 47.9 reduce-scatter.3
  205.3 29.4 reduce-scatter.5
  249.2 34.0 reduce-scatter.7
